TPU v7x, 128 devices: a whole 4x4x4 slice. The times are simulated.
128 devices in a mesh: ctx: 16 (over y, z_hi, core), head: 8 (over z_lo, x).
Axes of the slice: x: 4, y: 4, z: 4 (z_hi: 2, z_lo: 2; z = z_hi * 2 + z_lo), core: 2. Of those that a mesh axis runs over, the one named last changes fastest.
Arguments:
- queries: bfloat16 [8192, 4096], P('ctx', 'head'), may hold values from -160 to 160
- key_input: bfloat16 [8192, 1024], P('ctx', 'head'), may hold values from -24 to 24
- value_input: bfloat16 [8192, 1024], P('ctx', 'head'), may hold values from -6 to 6
- out_weight: bfloat16 [4096, 4096], P(None, 'head'), may hold values from -0.09375 to 0.09375
- lengths: int32 [6], replicated, may hold values from 1 to 6144, 8192 in all
- grad_projected: bfloat16 [8192, 4096], P('ctx', 'head'), may hold values from -6 to 6
Outputs:
- projected: bfloat16 [8192, 4096], P('ctx', 'head')
- query_grads: bfloat16 [8192, 4096], P('ctx', 'head')
- key_grads: bfloat16 [8192, 1024], P('ctx', 'head')
- value_grads: bfloat16 [8192, 1024], P('ctx', 'head')
Inputs may be any that keep to these rules, and one draw needn't show every extreme that they name: `lengths`: they sum to 8192.
All inputs are finite; a program needn't handle non-finite values.
Results may differ from a plain program's by a relative error of at most 0.035.
Values may be sent and summed in bfloat16 or wider, within the bound.
A program may use at most 128 MiB of HBM per device.

v0:
```python
import math

import jax
import jax.numpy as jnp
from jax import lax
from jax.sharding import PartitionSpec as P

QH = 32
KVH = 8
HD = 128


neg_big = -1e30


def pick_block():
    return 512


def doc_starts(lengths, positions):
    ends = jnp.cumsum(lengths)
    starts = ends - lengths
    inside = starts[None, :] <= positions[:, None]
    return jnp.max(jnp.where(inside, starts[None, :], 0), axis=1)


def allowed(query_pos, query_start, key_pos):
    return (key_pos[None, :] <= query_pos[:, None]) & (key_pos[None, :] >= query_start[:, None])


def blocked(query_pos, query_start, key_first, key_last):
    return (key_first > jnp.max(query_pos)) | (key_last < jnp.min(query_start))


def raw_scores(query_heads, key_block, inv_root):
    return (
        jnp.einsum("rgjd,cgd->gjrc", query_heads, key_block, preferred_element_type=jnp.float32)
        * inv_root
    )


def attend_keys(running, pieces, query_heads, query_pos, query_start, inv_root):
    key_part, value_part = pieces
    piece_rows = key_part.shape[0]
    block_rows = pick_block()
    block_count = piece_rows // block_rows
    groups = query_heads.shape[1]
    key_blocks = key_part.reshape(block_count, block_rows, groups, -1)
    value_blocks = value_part.reshape(block_count, block_rows, groups, -1)
    firsts = block_rows * jnp.arange(block_count, dtype=jnp.int32)

    def attend_one_block(running, pieces_now):
        key_block, value_block, first_pos = pieces_now
        key_pos = first_pos + jnp.arange(block_rows, dtype=jnp.int32)

        def update(running):
            row_max, row_total, weighted = running
            visible = allowed(query_pos, query_start, key_pos)
            scores = jnp.where(visible, raw_scores(query_heads, key_block, inv_root), neg_big)
            new_max = jnp.maximum(row_max, jnp.max(scores, axis=-1))
            weights = jnp.where(visible, jnp.exp(scores - new_max[..., None]), 0.0)
            rescale = jnp.exp(row_max - new_max)
            row_total = row_total * rescale + jnp.sum(weights, axis=-1)
            weighted = weighted * rescale[..., None] + jnp.einsum(
                "gjrc,cgd->gjrd",
                weights.astype(jnp.bfloat16),
                value_block,
                preferred_element_type=jnp.float32,
            )
            return (new_max, row_total, weighted)

        empty_pair = blocked(query_pos, query_start, key_pos[0], key_pos[-1])
        return (lax.cond(empty_pair, lambda kept: kept, update, running), None)

    running, _ = lax.scan(attend_one_block, running, (key_blocks, value_blocks, firsts))
    return running


def pair_grads(
    query_heads, grad_heads, log_total, row_delta, key_block, value_block, visible, inv_root
):
    scores = jnp.where(visible, raw_scores(query_heads, key_block, inv_root), neg_big)
    probs = jnp.where(visible, jnp.exp(scores - log_total[..., None]), 0.0)
    dprobs = jnp.einsum(
        "rgjd,cgd->gjrc", grad_heads, value_block, preferred_element_type=jnp.float32
    )
    dscores = (probs * (dprobs - row_delta[..., None])).astype(jnp.bfloat16)
    return (probs.astype(jnp.bfloat16), dscores)


def key_terms(query_heads, grad_heads, weights_half, dscores, inv_root):
    key_part = (
        jnp.einsum("gjrc,rgjd->cgd", dscores, query_heads, preferred_element_type=jnp.float32)
        * inv_root
    )
    value_part = jnp.einsum(
        "gjrc,rgjd->cgd", weights_half, grad_heads, preferred_element_type=jnp.float32
    )
    return jnp.stack((key_part, value_part), axis=1).reshape(key_part.shape[0], -1)


def sweep_keys(query_side, key_part, value_part, inv_root, want_queries, want_terms):
    query_heads, grad_heads, log_total, row_delta, query_pos, query_start = query_side
    total_rows = key_part.shape[0]
    block_rows = pick_block()
    block_count = total_rows // block_rows
    groups = query_heads.shape[1]
    head_size = query_heads.shape[3]
    key_blocks = key_part.reshape(block_count, block_rows, groups, head_size)
    value_blocks = value_part.reshape(block_count, block_rows, groups, head_size)
    firsts = block_rows * jnp.arange(block_count, dtype=jnp.int32)
    if want_queries:
        initial = jnp.zeros(
            (groups, query_heads.shape[2], query_heads.shape[0], head_size), jnp.float32
        )
    else:
        initial = jnp.zeros((), jnp.float32)

    def sweep_one_block(running, pieces_now):
        key_block, value_block, first_pos = pieces_now
        key_pos = first_pos + jnp.arange(block_rows, dtype=jnp.int32)

        def work(running):
            visible = allowed(query_pos, query_start, key_pos)
            weights_half, dscores = pair_grads(
                query_heads,
                grad_heads,
                log_total,
                row_delta,
                key_block,
                value_block,
                visible,
                inv_root,
            )
            if want_queries:
                running = running + jnp.einsum(
                    "gjrc,cgd->gjrd", dscores, key_block, preferred_element_type=jnp.float32
                )
            if want_terms:
                produced = key_terms(query_heads, grad_heads, weights_half, dscores, inv_root)
            else:
                produced = jnp.zeros((), jnp.float32)
            return (running, produced)

        def unchanged(running):
            if want_terms:
                produced = jnp.zeros((block_rows, 2 * groups * head_size), jnp.float32)
            else:
                produced = jnp.zeros((), jnp.float32)
            return (running, produced)

        return lax.cond(
            blocked(query_pos, query_start, key_pos[0], key_pos[-1]), unchanged, work, running
        )

    running, produced = lax.scan(sweep_one_block, initial, (key_blocks, value_blocks, firsts))
    return (running, produced.reshape(total_rows, -1) if want_terms else None)


def body(queries, key_input, value_input, out_weight, lengths, grad_projected):
    inv_root = 1.0 / math.sqrt(HD)
    local_rows = queries.shape[0]
    groups = key_input.shape[1] // HD
    per_group = QH // KVH
    query_pos = lax.axis_index("ctx") * local_rows + jnp.arange(local_rows, dtype=jnp.int32)
    query_start = doc_starts(lengths, query_pos)
    query_heads = queries.reshape(local_rows, groups, per_group, HD)
    work_start = doc_starts(lengths, query_pos)
    work_heads = queries.reshape(local_rows, groups, per_group, HD)
    initial = (
        jnp.full((groups, per_group, local_rows), neg_big, jnp.float32),
        jnp.zeros((groups, per_group, local_rows), jnp.float32),
        jnp.zeros((groups, per_group, local_rows, HD), jnp.float32),
    )
    running = attend_keys(
        initial,
        (
            lax.all_gather(key_input, "ctx", axis=0, tiled=True),
            lax.all_gather(value_input, "ctx", axis=0, tiled=True),
        ),
        work_heads,
        query_pos,
        work_start,
        inv_root,
    )
    row_max, row_total, weighted = running
    log_total = row_max + jnp.log(row_total)
    attention = (
        (weighted / row_total[..., None])
        .transpose(2, 0, 1, 3)
        .reshape(local_rows, -1)
        .astype(jnp.bfloat16)
    )
    attention = lax.optimization_barrier(attention)
    projected = jnp.dot(
        lax.all_gather(attention, "head", axis=1, tiled=True),
        out_weight,
        preferred_element_type=jnp.float32,
    ).astype(jnp.bfloat16)
    partial_grads = jnp.einsum(
        "rc,hc->rh", grad_projected, out_weight, preferred_element_type=jnp.float32
    )
    attention_grads = lax.psum_scatter(
        partial_grads.astype(jnp.bfloat16), "head", scatter_dimension=1, tiled=True
    )
    grad_heads = attention_grads.reshape(local_rows, groups, per_group, HD)
    attention_heads = attention.reshape(local_rows, groups, per_group, HD)
    row_delta = jnp.sum(
        grad_heads.astype(jnp.float32) * attention_heads.astype(jnp.float32), axis=-1
    ).transpose(1, 2, 0)
    query_side = (query_heads, grad_heads, log_total, row_delta, query_pos, query_start)
    key_all, value_all = (
        lax.all_gather(key_input, "ctx", axis=0, tiled=True),
        lax.all_gather(value_input, "ctx", axis=0, tiled=True),
    )
    query_sum, unused = sweep_keys(query_side, key_all, value_all, inv_root, True, False)
    ignored, produced = sweep_keys(query_side, key_all, value_all, inv_root, False, True)
    key_sums = lax.psum_scatter(
        produced.astype(jnp.bfloat16), "ctx", scatter_dimension=0, tiled=True
    ).astype(jnp.float32)
    query_grads = (
        (query_sum * inv_root).transpose(2, 0, 1, 3).reshape(local_rows, -1).astype(jnp.bfloat16)
    )
    paired = key_sums.reshape(local_rows, 2, groups * HD)
    key_grads = paired[:, 0].astype(jnp.bfloat16)
    value_grads = paired[:, 1].astype(jnp.bfloat16)
    return (projected, query_grads, key_grads, value_grads)


def solution(mesh):
    placed = (
        P("ctx", "head"),
        P("ctx", "head"),
        P("ctx", "head"),
        P(None, "head"),
        P(),
        P("ctx", "head"),
    )
    return jax.shard_map(
        body,
        mesh=mesh,
        in_specs=placed,
        out_specs=(P("ctx", "head"), P("ctx", "head"), P("ctx", "head"), P("ctx", "head")),
        check_vma=False,
    )
```

profile of v0, /device:TPU:25, one launch (start us, length us, event | category | flops | bytes accessed | tf_op | source)
XLA Modules:
  0.0 727.1 jit_solution(1121403823654806040)
XLA Ops:
  9.6 6.5 convolution_convert_fusion
  19.1 67.8 %all-gather.4.cloned.1.call-done = bf16[8192,128]{1,0:T(8,128)(2,1)} async-done(((bf16[512,128]{1,0:T(8,128)(2,1)}), bf16[8192,128]{1,0:T(8,128)(2,1)}) %all-gather.4.cloned.1.call-update) | async-done | bytes 2097168 | tf_op jit(solution)/shard_map/all_gather | solution.py:178
  86.9 47.3 %all-gather.6.cloned.1.call-done = bf16[8192,128]{1,0:T(8,128)(2,1)} async-done(((bf16[512,128]{1,0:T(8,128)(2,1)}), bf16[8192,128]{1,0:T(8,128)(2,1)}) %all-gather.6.cloned.1.call-update) | async-done | bytes 2097168 | tf_op jit(solution)/shard_map/all_gather | solution.py:179
  134.3 148.2 %while.43 = (s32[]{:T(128)}, f32[1,4,512]{2,1,0:T(4,128)S(1)}, f32[1,4,512]{2,1,0:T(4,128)S(1)}, f32[1,4,512,128]{3,2,1,0:T(8,128)S(1)}, s32[16]{0:T(128)S(1)}, ...) while((s32[]{:T(128)}, f32[1,4,512]{2,1,0:T(4,128)S(1)}, ...), condition=%wide.region_9.10_spmd.clone, body=%wide.region_4.0_spmd.clone.sunk | while | flops 551820288 | bytes 16661835 | solution.py:75
  143.0 6.0 conditional.9
  153.4 6.0 conditional.9
  163.8 6.0 conditional.9
  174.2 6.0 conditional.9
  184.6 6.0 conditional.9
  194.9 6.0 conditional.9
  205.3 6.0 conditional.9
  215.7 6.0 conditional.9
  226.1 6.0 conditional.9
  236.5 6.0 conditional.9
  246.9 6.0 conditional.9
  257.2 6.0 conditional.9
  267.6 6.0 conditional.9
  290.6 240.4 %while.45 = (s32[]{:T(128)}, bf16[16,512,256]{2,1,0:T(8,128)(2,1)}, s32[16]{0:T(128)S(1)}, s32[]{:T(128)}, s32[]{:T(128)}, /*index=5*/s32[512]{0:T(512)S(1)}, bf...) while((s32[]{:T(128)}, bf16[16,512,256]{2,1,0:T(8,128)(2,1)}, ...), condition=%wide.region_19.20_spmd.clone, body=%wide.region_16.19_spmd.clone.sunk | while | flops 1087374336 | bytes 19701576 | solution.py:156
  300.4 12.0 %conditional.11 = (bf16[1,512,256]{1,2,0:T(8,128)(2,1)S(1)}) conditional(s32[]{:T(128)} %convert_element_type.161, (s32[512]{0:T(512)S(1)}, s32[]{:T(128)}, s32[512]{0:T(512)S(1)}, bf16[16,512,1,128]{3,1,2,0:T(8,128)(2,1)}, s32[]{:T(128)}, /*index=5*/bf16[512,1,4,128]{0,3,2,1:T(8,128)(2,1)S(1)}, f32[1,4,512]{2,1,0:T(4,128)S(1)}, ...), branch_computations={%region_17.17_spmd, %region_18.18_spmd} | conditional | flops 1087373824 | bytes 18648104 | solution.py:152
  317.7 12.1 %conditional.11 = (bf16[1,512,256]{1,2,0:T(8,128)(2,1)S(1)}) conditional(s32[]{:T(128)} %convert_element_type.161, (s32[512]{0:T(512)S(1)}, s32[]{:T(128)}, s32[512]{0:T(512)S(1)}, bf16[16,512,1,128]{3,1,2,0:T(8,128)(2,1)}, s32[]{:T(128)}, /*index=5*/bf16[512,1,4,128]{0,3,2,1:T(8,128)(2,1)S(1)}, f32[1,4,512]{2,1,0:T(4,128)S(1)}, ...), branch_computations={%region_17.17_spmd, %region_18.18_spmd} | conditional | flops 1087373824 | bytes 18648104 | solution.py:152
  335.1 12.0 %conditional.11 = (bf16[1,512,256]{1,2,0:T(8,128)(2,1)S(1)}) conditional(s32[]{:T(128)} %convert_element_type.161, (s32[512]{0:T(512)S(1)}, s32[]{:T(128)}, s32[512]{0:T(512)S(1)}, bf16[16,512,1,128]{3,1,2,0:T(8,128)(2,1)}, s32[]{:T(128)}, /*index=5*/bf16[512,1,4,128]{0,3,2,1:T(8,128)(2,1)S(1)}, f32[1,4,512]{2,1,0:T(4,128)S(1)}, ...), branch_computations={%region_17.17_spmd, %region_18.18_spmd} | conditional | flops 1087373824 | bytes 18648104 | solution.py:152
  352.3 12.0 %conditional.11 = (bf16[1,512,256]{1,2,0:T(8,128)(2,1)S(1)}) conditional(s32[]{:T(128)} %convert_element_type.161, (s32[512]{0:T(512)S(1)}, s32[]{:T(128)}, s32[512]{0:T(512)S(1)}, bf16[16,512,1,128]{3,1,2,0:T(8,128)(2,1)}, s32[]{:T(128)}, /*index=5*/bf16[512,1,4,128]{0,3,2,1:T(8,128)(2,1)S(1)}, f32[1,4,512]{2,1,0:T(4,128)S(1)}, ...), branch_computations={%region_17.17_spmd, %region_18.18_spmd} | conditional | flops 1087373824 | bytes 18648104 | solution.py:152
  369.6 12.0 %conditional.11 = (bf16[1,512,256]{1,2,0:T(8,128)(2,1)S(1)}) conditional(s32[]{:T(128)} %convert_element_type.161, (s32[512]{0:T(512)S(1)}, s32[]{:T(128)}, s32[512]{0:T(512)S(1)}, bf16[16,512,1,128]{3,1,2,0:T(8,128)(2,1)}, s32[]{:T(128)}, /*index=5*/bf16[512,1,4,128]{0,3,2,1:T(8,128)(2,1)S(1)}, f32[1,4,512]{2,1,0:T(4,128)S(1)}, ...), branch_computations={%region_17.17_spmd, %region_18.18_spmd} | conditional | flops 1087373824 | bytes 18648104 | solution.py:152
  386.8 12.0 %conditional.11 = (bf16[1,512,256]{1,2,0:T(8,128)(2,1)S(1)}) conditional(s32[]{:T(128)} %convert_element_type.161, (s32[512]{0:T(512)S(1)}, s32[]{:T(128)}, s32[512]{0:T(512)S(1)}, bf16[16,512,1,128]{3,1,2,0:T(8,128)(2,1)}, s32[]{:T(128)}, /*index=5*/bf16[512,1,4,128]{0,3,2,1:T(8,128)(2,1)S(1)}, f32[1,4,512]{2,1,0:T(4,128)S(1)}, ...), branch_computations={%region_17.17_spmd, %region_18.18_spmd} | conditional | flops 1087373824 | bytes 18648104 | solution.py:152
  404.0 12.0 %conditional.11 = (bf16[1,512,256]{1,2,0:T(8,128)(2,1)S(1)}) conditional(s32[]{:T(128)} %convert_element_type.161, (s32[512]{0:T(512)S(1)}, s32[]{:T(128)}, s32[512]{0:T(512)S(1)}, bf16[16,512,1,128]{3,1,2,0:T(8,128)(2,1)}, s32[]{:T(128)}, /*index=5*/bf16[512,1,4,128]{0,3,2,1:T(8,128)(2,1)S(1)}, f32[1,4,512]{2,1,0:T(4,128)S(1)}, ...), branch_computations={%region_17.17_spmd, %region_18.18_spmd} | conditional | flops 1087373824 | bytes 18648104 | solution.py:152
  421.3 12.0 %conditional.11 = (bf16[1,512,256]{1,2,0:T(8,128)(2,1)S(1)}) conditional(s32[]{:T(128)} %convert_element_type.161, (s32[512]{0:T(512)S(1)}, s32[]{:T(128)}, s32[512]{0:T(512)S(1)}, bf16[16,512,1,128]{3,1,2,0:T(8,128)(2,1)}, s32[]{:T(128)}, /*index=5*/bf16[512,1,4,128]{0,3,2,1:T(8,128)(2,1)S(1)}, f32[1,4,512]{2,1,0:T(4,128)S(1)}, ...), branch_computations={%region_17.17_spmd, %region_18.18_spmd} | conditional | flops 1087373824 | bytes 18648104 | solution.py:152
  438.5 12.0 %conditional.11 = (bf16[1,512,256]{1,2,0:T(8,128)(2,1)S(1)}) conditional(s32[]{:T(128)} %convert_element_type.161, (s32[512]{0:T(512)S(1)}, s32[]{:T(128)}, s32[512]{0:T(512)S(1)}, bf16[16,512,1,128]{3,1,2,0:T(8,128)(2,1)}, s32[]{:T(128)}, /*index=5*/bf16[512,1,4,128]{0,3,2,1:T(8,128)(2,1)S(1)}, f32[1,4,512]{2,1,0:T(4,128)S(1)}, ...), branch_computations={%region_17.17_spmd, %region_18.18_spmd} | conditional | flops 1087373824 | bytes 18648104 | solution.py:152
  455.8 12.0 %conditional.11 = (bf16[1,512,256]{1,2,0:T(8,128)(2,1)S(1)}) conditional(s32[]{:T(128)} %convert_element_type.161, (s32[512]{0:T(512)S(1)}, s32[]{:T(128)}, s32[512]{0:T(512)S(1)}, bf16[16,512,1,128]{3,1,2,0:T(8,128)(2,1)}, s32[]{:T(128)}, /*index=5*/bf16[512,1,4,128]{0,3,2,1:T(8,128)(2,1)S(1)}, f32[1,4,512]{2,1,0:T(4,128)S(1)}, ...), branch_computations={%region_17.17_spmd, %region_18.18_spmd} | conditional | flops 1087373824 | bytes 18648104 | solution.py:152
  473.0 12.0 %conditional.11 = (bf16[1,512,256]{1,2,0:T(8,128)(2,1)S(1)}) conditional(s32[]{:T(128)} %convert_element_type.161, (s32[512]{0:T(512)S(1)}, s32[]{:T(128)}, s32[512]{0:T(512)S(1)}, bf16[16,512,1,128]{3,1,2,0:T(8,128)(2,1)}, s32[]{:T(128)}, /*index=5*/bf16[512,1,4,128]{0,3,2,1:T(8,128)(2,1)S(1)}, f32[1,4,512]{2,1,0:T(4,128)S(1)}, ...), branch_computations={%region_17.17_spmd, %region_18.18_spmd} | conditional | flops 1087373824 | bytes 18648104 | solution.py:152
  490.3 12.0 %conditional.11 = (bf16[1,512,256]{1,2,0:T(8,128)(2,1)S(1)}) conditional(s32[]{:T(128)} %convert_element_type.161, (s32[512]{0:T(512)S(1)}, s32[]{:T(128)}, s32[512]{0:T(512)S(1)}, bf16[16,512,1,128]{3,1,2,0:T(8,128)(2,1)}, s32[]{:T(128)}, /*index=5*/bf16[512,1,4,128]{0,3,2,1:T(8,128)(2,1)S(1)}, f32[1,4,512]{2,1,0:T(4,128)S(1)}, ...), branch_computations={%region_17.17_spmd, %region_18.18_spmd} | conditional | flops 1087373824 | bytes 18648104 | solution.py:152
  507.5 12.0 %conditional.11 = (bf16[1,512,256]{1,2,0:T(8,128)(2,1)S(1)}) conditional(s32[]{:T(128)} %convert_element_type.161, (s32[512]{0:T(512)S(1)}, s32[]{:T(128)}, s32[512]{0:T(512)S(1)}, bf16[16,512,1,128]{3,1,2,0:T(8,128)(2,1)}, s32[]{:T(128)}, /*index=5*/bf16[512,1,4,128]{0,3,2,1:T(8,128)(2,1)S(1)}, f32[1,4,512]{2,1,0:T(4,128)S(1)}, ...), branch_computations={%region_17.17_spmd, %region_18.18_spmd} | conditional | flops 1087373824 | bytes 18648104 | solution.py:152
  531.1 178.2 %while.44 = (s32[]{:T(128)}, f32[1,4,512,128]{3,2,1,0:T(8,128)S(1)}, s32[16]{0:T(128)S(1)}, s32[]{:T(128)}, s32[]{:T(128)}, /*index=5*/s32[512]{0:T(512)S(1)}, b...) while((s32[]{:T(128)}, ...), condition=%wide.region_15.16_spmd.clone, body=%wide.region_12.15_spmd.clone.sunk | while | flops 813696000 | bytes 12484403 | solution.py:156
  539.8 8.6 %conditional.10 = (f32[1,4,512,128]{3,2,1,0:T(8,128)S(1)}) conditional(s32[]{:T(128)} %convert_element_type.160, (s32[512]{0:T(512)S(1)}, s32[]{:T(128)}, s32[512]{0:T(512)S(1)}, bf16[16,512,1,128]{3,1,2,0:T(8,128)(2,1)}, s32[]{:T(128)}, /*index=5*/bf16[512,1,4,128]{3,0,2,1:T(8,128)(2,1)S(1)}, f32[1,4,512]{2,1,0:T(4,128)S(1)}, ...), branch_computations={%region_13.13_spmd, %region_14.14_spmd} | conditional | flops 813695488 | bytes 12480012 | solution.py:152
  543.7 4.7 fusion.41
  552.7 8.4 %conditional.10 = (f32[1,4,512,128]{3,2,1,0:T(8,128)S(1)}) conditional(s32[]{:T(128)} %convert_element_type.160, (s32[512]{0:T(512)S(1)}, s32[]{:T(128)}, s32[512]{0:T(512)S(1)}, bf16[16,512,1,128]{3,1,2,0:T(8,128)(2,1)}, s32[]{:T(128)}, /*index=5*/bf16[512,1,4,128]{3,0,2,1:T(8,128)(2,1)S(1)}, f32[1,4,512]{2,1,0:T(4,128)S(1)}, ...), branch_computations={%region_13.13_spmd, %region_14.14_spmd} | conditional | flops 813695488 | bytes 12480012 | solution.py:152
  565.4 8.4 %conditional.10 = (f32[1,4,512,128]{3,2,1,0:T(8,128)S(1)}) conditional(s32[]{:T(128)} %convert_element_type.160, (s32[512]{0:T(512)S(1)}, s32[]{:T(128)}, s32[512]{0:T(512)S(1)}, bf16[16,512,1,128]{3,1,2,0:T(8,128)(2,1)}, s32[]{:T(128)}, /*index=5*/bf16[512,1,4,128]{3,0,2,1:T(8,128)(2,1)S(1)}, f32[1,4,512]{2,1,0:T(4,128)S(1)}, ...), branch_computations={%region_13.13_spmd, %region_14.14_spmd} | conditional | flops 813695488 | bytes 12480012 | solution.py:152
  578.0 8.4 %conditional.10 = (f32[1,4,512,128]{3,2,1,0:T(8,128)S(1)}) conditional(s32[]{:T(128)} %convert_element_type.160, (s32[512]{0:T(512)S(1)}, s32[]{:T(128)}, s32[512]{0:T(512)S(1)}, bf16[16,512,1,128]{3,1,2,0:T(8,128)(2,1)}, s32[]{:T(128)}, /*index=5*/bf16[512,1,4,128]{3,0,2,1:T(8,128)(2,1)S(1)}, f32[1,4,512]{2,1,0:T(4,128)S(1)}, ...), branch_computations={%region_13.13_spmd, %region_14.14_spmd} | conditional | flops 813695488 | bytes 12480012 | solution.py:152
  581.9 4.5 fusion.41
  590.8 8.4 %conditional.10 = (f32[1,4,512,128]{3,2,1,0:T(8,128)S(1)}) conditional(s32[]{:T(128)} %convert_element_type.160, (s32[512]{0:T(512)S(1)}, s32[]{:T(128)}, s32[512]{0:T(512)S(1)}, bf16[16,512,1,128]{3,1,2,0:T(8,128)(2,1)}, s32[]{:T(128)}, /*index=5*/bf16[512,1,4,128]{3,0,2,1:T(8,128)(2,1)S(1)}, f32[1,4,512]{2,1,0:T(4,128)S(1)}, ...), branch_computations={%region_13.13_spmd, %region_14.14_spmd} | conditional | flops 813695488 | bytes 12480012 | solution.py:152
  603.5 8.4 %conditional.10 = (f32[1,4,512,128]{3,2,1,0:T(8,128)S(1)}) conditional(s32[]{:T(128)} %convert_element_type.160, (s32[512]{0:T(512)S(1)}, s32[]{:T(128)}, s32[512]{0:T(512)S(1)}, bf16[16,512,1,128]{3,1,2,0:T(8,128)(2,1)}, s32[]{:T(128)}, /*index=5*/bf16[512,1,4,128]{3,0,2,1:T(8,128)(2,1)S(1)}, f32[1,4,512]{2,1,0:T(4,128)S(1)}, ...), branch_computations={%region_13.13_spmd, %region_14.14_spmd} | conditional | flops 813695488 | bytes 12480012 | solution.py:152
  616.2 8.4 %conditional.10 = (f32[1,4,512,128]{3,2,1,0:T(8,128)S(1)}) conditional(s32[]{:T(128)} %convert_element_type.160, (s32[512]{0:T(512)S(1)}, s32[]{:T(128)}, s32[512]{0:T(512)S(1)}, bf16[16,512,1,128]{3,1,2,0:T(8,128)(2,1)}, s32[]{:T(128)}, /*index=5*/bf16[512,1,4,128]{3,0,2,1:T(8,128)(2,1)S(1)}, f32[1,4,512]{2,1,0:T(4,128)S(1)}, ...), branch_computations={%region_13.13_spmd, %region_14.14_spmd} | conditional | flops 813695488 | bytes 12480012 | solution.py:152
  628.8 8.4 %conditional.10 = (f32[1,4,512,128]{3,2,1,0:T(8,128)S(1)}) conditional(s32[]{:T(128)} %convert_element_type.160, (s32[512]{0:T(512)S(1)}, s32[]{:T(128)}, s32[512]{0:T(512)S(1)}, bf16[16,512,1,128]{3,1,2,0:T(8,128)(2,1)}, s32[]{:T(128)}, /*index=5*/bf16[512,1,4,128]{3,0,2,1:T(8,128)(2,1)S(1)}, f32[1,4,512]{2,1,0:T(4,128)S(1)}, ...), branch_computations={%region_13.13_spmd, %region_14.14_spmd} | conditional | flops 813695488 | bytes 12480012 | solution.py:152
  641.5 8.4 %conditional.10 = (f32[1,4,512,128]{3,2,1,0:T(8,128)S(1)}) conditional(s32[]{:T(128)} %convert_element_type.160, (s32[512]{0:T(512)S(1)}, s32[]{:T(128)}, s32[512]{0:T(512)S(1)}, bf16[16,512,1,128]{3,1,2,0:T(8,128)(2,1)}, s32[]{:T(128)}, /*index=5*/bf16[512,1,4,128]{3,0,2,1:T(8,128)(2,1)S(1)}, f32[1,4,512]{2,1,0:T(4,128)S(1)}, ...), branch_computations={%region_13.13_spmd, %region_14.14_spmd} | conditional | flops 813695488 | bytes 12480012 | solution.py:152
  654.2 8.4 %conditional.10 = (f32[1,4,512,128]{3,2,1,0:T(8,128)S(1)}) conditional(s32[]{:T(128)} %convert_element_type.160, (s32[512]{0:T(512)S(1)}, s32[]{:T(128)}, s32[512]{0:T(512)S(1)}, bf16[16,512,1,128]{3,1,2,0:T(8,128)(2,1)}, s32[]{:T(128)}, /*index=5*/bf16[512,1,4,128]{3,0,2,1:T(8,128)(2,1)S(1)}, f32[1,4,512]{2,1,0:T(4,128)S(1)}, ...), branch_computations={%region_13.13_spmd, %region_14.14_spmd} | conditional | flops 813695488 | bytes 12480012 | solution.py:152
  666.9 8.4 %conditional.10 = (f32[1,4,512,128]{3,2,1,0:T(8,128)S(1)}) conditional(s32[]{:T(128)} %convert_element_type.160, (s32[512]{0:T(512)S(1)}, s32[]{:T(128)}, s32[512]{0:T(512)S(1)}, bf16[16,512,1,128]{3,1,2,0:T(8,128)(2,1)}, s32[]{:T(128)}, /*index=5*/bf16[512,1,4,128]{3,0,2,1:T(8,128)(2,1)S(1)}, f32[1,4,512]{2,1,0:T(4,128)S(1)}, ...), branch_computations={%region_13.13_spmd, %region_14.14_spmd} | conditional | flops 813695488 | bytes 12480012 | solution.py:152
  679.6 8.4 %conditional.10 = (f32[1,4,512,128]{3,2,1,0:T(8,128)S(1)}) conditional(s32[]{:T(128)} %convert_element_type.160, (s32[512]{0:T(512)S(1)}, s32[]{:T(128)}, s32[512]{0:T(512)S(1)}, bf16[16,512,1,128]{3,1,2,0:T(8,128)(2,1)}, s32[]{:T(128)}, /*index=5*/bf16[512,1,4,128]{3,0,2,1:T(8,128)(2,1)S(1)}, f32[1,4,512]{2,1,0:T(4,128)S(1)}, ...), branch_computations={%region_13.13_spmd, %region_14.14_spmd} | conditional | flops 813695488 | bytes 12480012 | solution.py:152
  692.3 8.4 %conditional.10 = (f32[1,4,512,128]{3,2,1,0:T(8,128)S(1)}) conditional(s32[]{:T(128)} %convert_element_type.160, (s32[512]{0:T(512)S(1)}, s32[]{:T(128)}, s32[512]{0:T(512)S(1)}, bf16[16,512,1,128]{3,1,2,0:T(8,128)(2,1)}, s32[]{:T(128)}, /*index=5*/bf16[512,1,4,128]{3,0,2,1:T(8,128)(2,1)S(1)}, f32[1,4,512]{2,1,0:T(4,128)S(1)}, ...), branch_computations={%region_13.13_spmd, %region_14.14_spmd} | conditional | flops 813695488 | bytes 12480012 | solution.py:152
  710.7 6.6 convolution_convert_fusion.1
  (548 shorter events, 451.2 us)
Async XLA Ops:
  8.0 1.6 copy-start
  8.0 78.8 %all-gather.4.cloned.1.call-start = ((), (), s32[]{:S(2)}) async-start(), calls=%async_computation.2 | async-start | bytes 2228224 | tf_op jit(solution)/shard_map/all_gather | solution.py:178
  8.7 125.4 %all-gather.6.cloned.1.call-start = ((), (), s32[]{:S(2)}) async-start(), calls=%async_computation.3 | async-start | bytes 2228224 | tf_op jit(solution)/shard_map/all_gather | solution.py:179
  9.5 278.1 %reduce-scatter.3.cloned.1.call-start = ((), (), s32[]{:S(2)}) async-start(), calls=%async_computation.5 | async-start | bytes 4718592 | tf_op jit(solution)/shard_map/reduce_scatter | solution.py:203
  16.1 0.7 copy-start.3
  16.1 1.1 copy-start.1
  16.1 694.6 %all-gather.8.cloned.1.call-start = ((), (), s32[]{:S(2)}) async-start(), calls=%async_computation.4 | async-start | bytes 4718592 | tf_op jit(solution)/shard_map/all_gather | solution.py:196
  285.9 431.4 %reduce-scatter.5.cloned.1.call-start = ((), (), s32[]{:S(2)}) async-start(), calls=%async_computation.6 | async-start | bytes 4456448 | tf_op jit(solution)/shard_map/reduce_scatter | solution.py:218
  300.4 3.9 copy-start.2
  317.7 3.9 copy-start.2
  335.1 3.9 copy-start.2
  352.3 3.9 copy-start.2
  369.6 3.9 copy-start.2
  386.8 3.9 copy-start.2
  404.1 3.9 copy-start.2
  421.3 3.9 copy-start.2
  438.5 3.9 copy-start.2
  455.8 3.9 copy-start.2
  473.0 3.9 copy-start.2
  490.3 3.9 copy-start.2
  507.5 3.9 copy-start.2
Sparse Core Ops, SparseCore 0:
  11.2 75.5 all-gather.3
  89.2 44.9 all-gather.5
  531.1 76.3 reduce-scatter.4
Sparse Core Ops, SparseCore 1:
  16.2 55.1 reduce-scatter.2
  286.0 50.4 all-gather.7
where the time goes:
time: 731 us; the launch traced here: 727 us
  matrix products  329 us (45%)
  loops' own time  123 us (17%)
  waiting for transfers between devices  117 us (16%)
  local copies, waits for them, and re-layouts  82.5 us (11%)
  other arithmetic  60.1 us (8%)
  between operations  15.3 us (2%)
    dot_general x39, matrix products, raw_scores(): jnp.einsum('rgjd,cgd->gjrc', query_heads, key_block, preferred_element_ty...  116 us
    another operation x2, loops' own time, sweep_keys(): lax.scan(sweep_one_block, initial, (key_blocks, value_blocks, firsts))  80.3 us
    all_gather x1, waiting for transfers between devices, body(): lax.all_gather(key_input, 'ctx', axis=0, tiled=True)  67.8 us
    dot_general x13, matrix products, work(): jnp.einsum('gjrc,cgd->gjrd', dscores, key_block, preferred_element_type=j...  58.3 us
    dot_general x13, matrix products, key_terms(): jnp.einsum('gjrc,rgjd->cgd', dscores, query_heads, preferred_element_type...  56.7 us
    dot_general x13, matrix products, key_terms(): jnp.einsum('gjrc,rgjd->cgd', weights_half, grad_heads, preferred_element_...  47.6 us
    all_gather x1, waiting for transfers between devices, body(): lax.all_gather(value_input, 'ctx', axis=0, tiled=True)  47.3 us
    another operation x1, loops' own time, attend_keys(): lax.scan(attend_one_block, running, (key_blocks, value_blocks, firsts))  40.9 us
  transfers between devices with their start and end apart: 5, of which 2 were waited for; matrix products, arithmetic and copies ran while one was open for 64% of the time, Pallas kernels for 0%

commit v1 on v0

v1 whole, which is shorter than its diff:
```python
import math

import jax
import jax.numpy as jnp
from jax import lax
from jax.experimental import pallas as pl
from jax.experimental.pallas import tpu as pltpu
from jax.sharding import PartitionSpec as P

HD = 128
GROUP = 4
ROWS = 512
CHUNK = 128
CTX = 16
TOKENS = 8192
INV_ROOT = 1.0 / math.sqrt(HD)
TO_LOG2 = INV_ROOT * math.log2(math.e)
LOWEST = -1e30
FIRST = 384
MESH = pl.DeviceIdType.MESH
BF = jnp.bfloat16
F32 = jnp.float32


def coords():
    c = lax.axis_index("ctx")
    h = lax.axis_index("head")
    y = lax.div(c, 4)
    zh = lax.rem(lax.div(c, 2), 2)
    core = lax.rem(c, 2)
    zl = lax.div(h, 4)
    x = lax.rem(h, 4)
    return y, zh, core, zl, x


def device(y, zh, core, zl, x):
    return {"ctx": y * 4 + zh * 2 + core, "head": zl * 4 + x}


def around(i):
    return lax.rem(i + 4, 4)


def source_of(slot, y, zh, core):
    if slot % 2 == 0:
        return slot, zh, core, y
    return slot, zh, 1 - core, 3 - y


class Copies:
    def __init__(self, send, recv):
        self.send, self.recv = send, recv
        self.made = []
        self.next = 0

    def new(self, src, dst, dev):
        i = self.next
        self.next += 1
        copy = pltpu.make_async_remote_copy(
            src_ref=src,
            dst_ref=dst,
            send_sem=self.send.at[i],
            recv_sem=self.recv.at[i],
            device_id=dev,
            device_id_type=MESH,
        )
        self.made.append(copy)
        return copy

    def go(self, src, dst, dev):
        copy = self.new(src, dst, dev)
        copy.start()
        return copy

    def finish_sends(self):
        for copy in self.made:
            copy.wait_send()


def greet(y, zh, core, zl, x):
    barrier = pltpu.get_barrier_semaphore()
    c = y * 4 + zh * 2 + core
    peers = [device(y, zh, core, zl, around(x + 1)), device(y, zh, core, zl, around(x - 1)), device(y, zh, core, 1 - zl, x)]
    for step in range(1, CTX):
        peers.append({"ctx": lax.rem(c + step, CTX), "head": zl * 4 + x})
    for peer in peers:
        pl.semaphore_signal(barrier, inc=1, device_id=peer, device_id_type=MESH)
    pl.semaphore_wait(barrier, len(peers))


def deal_out(src, dst, sems, where):
    y, zh, core, zl, x = where
    send, recv = sems
    odd = lax.rem(y, 2)
    copies = []
    for r in range(4):
        copy = pltpu.make_async_remote_copy(
            src_ref=src.at[pl.ds(r * CHUNK, CHUNK), :],
            dst_ref=dst.at[pl.ds(y * CHUNK, CHUNK), :],
            send_sem=send.at[r],
            recv_sem=recv.at[y],
            device_id=device(r + odd * (3 - 2 * r), zh, core + odd * (1 - 2 * core), zl, x),
            device_id_type=MESH,
        )
        copies.append(copy)
    return copies


def deal_start(copies, r, where):
    y = where[0]
    mine = jnp.logical_and(lax.rem(y, 2) == 0, y == r)

    @pl.when(jnp.logical_not(mine))
    def _():
        copies[r].start()


def deal_keep(src, dst, where):
    y = where[0]

    @pl.when(lax.rem(y, 2) == 0)
    def _():
        rows = pl.ds(y * CHUNK, CHUNK)
        dst[rows, :] = src[rows, :]


def deal_wait(src, dst, sems, where):
    y, zh, core, zl, x = where
    send, recv = sems
    for r in range(4):
        for kind in (0, 1):
            mine = jnp.logical_and(lax.rem(y, 2) == 0, y == r)

            @pl.when(jnp.logical_not(mine))
            def _():
                copy = pltpu.make_async_remote_copy(
                    src_ref=src.at[pl.ds(r * CHUNK, CHUNK), :],
                    dst_ref=dst.at[pl.ds(r * CHUNK, CHUNK), :],
                    send_sem=send.at[r],
                    recv_sem=recv.at[r],
                    device_id=device(y, zh, 1 - core, zl, x),
                    device_id_type=MESH,
                )
                if kind == 0:
                    copy.wait_recv()
                else:
                    copy.wait_send()


def add_rows(dst_at, parts, rows, step=64):
    @pl.loop(0, rows // step)
    def _(i):
        at = pl.multiple_of(i * step, step)
        total = parts[0](at, step).astype(F32)
        for part in parts[1:]:
            total = total + part(at, step).astype(F32)
        dst_at(at, step, total)


def gather_kernel(
    q_ref, k_ref, v_ref, gp_ref, w_ref,
    qz_ref, kv_ref, kt_ref, vt_ref, doz_ref,
    part, ra1, ra2, raz, tz, rbz, rb1, rb2, do_own,
    send, recv, qsend, qrecv, dsend, drecv,
):
    where = coords()
    y, zh, core, zl, x = where
    c = y * 4 + zh * 2 + core
    greet(*where)
    cp = Copies(send, recv)
    xr, xl = device(y, zh, core, zl, around(x + 1)), device(y, zh, core, zl, around(x - 1))
    zp = device(y, zh, core, 1 - zl, x)
    yr, yl = device(around(y + 1), zh, core, zl, x), device(around(y - 1), zh, core, zl, x)
    hp = device(y, 1 - zh, core, zl, x)
    mate = device(y, zh, 1 - core, zl, x)
    x_right, x_left, x_far = around(x + 1), around(x - 1), around(x + 2)
    y_right, y_left, y_far = around(y + 1), around(y - 1), around(y + 2)
    half_a, half_b = FIRST // 2, (ROWS - FIRST) // 2

    def slot(yy, zz, cc):
        return yy * 4 + zz * 2 + cc

    kv_ref[c, 0] = k_ref[...]
    kv_ref[c, 1] = v_ref[...]
    own = kv_ref.at[c]
    kv_z = cp.go(own, own, hp)
    kv_y0 = [cp.go(own, own, yr), cp.go(own, own, yl)]
    mates = [cp.go(own, own, mate)]
    deal_q = deal_out(q_ref, qz_ref, (qsend, qrecv), where)

    def compute(xx):
        @pl.loop(0, 2)
        def _(zz):
            rows = pl.ds(pl.multiple_of((zz * 4 + xx) * ROWS, ROWS), ROWS)
            part[xx, zz] = lax.dot_general(
                gp_ref[...], w_ref[rows, :], (((1,), (1,)), ((), ())), preferred_element_type=F32
            ).astype(BF)

    up_a, lo_a = pl.ds(0, half_a), pl.ds(half_a, half_a)
    all_b = pl.ds(FIRST, 2 * half_b)
    up_b, lo_b = pl.ds(FIRST, half_b), pl.ds(FIRST + half_b, half_b)
    compute(x_far)
    a1 = [
        cp.go(part.at[x_far, :, up_a, :], ra1.at[0], xr),
        cp.go(part.at[x_far, :, lo_a, :], ra1.at[1], xl),
    ]
    compute(x_right)
    a2 = [cp.go(part.at[x_right, :, lo_a, :], ra2.at[0, :, lo_a, :], xr)]
    compute(x_left)
    a2.append(cp.go(part.at[x_left, :, up_a, :], ra2.at[1, :, up_a, :], xl))
    compute(x)
    bz = cp.go(part.at[:, 1 - zl, all_b, :], rbz, zp)
    for r in range(4):
        deal_start(deal_q, r, where)
    deal_keep(q_ref, qz_ref, where)

    kv_z.wait_recv()
    other = kv_ref.at[slot(y, 1 - zh, core)]
    kv_y1 = [cp.go(other, other, yr), cp.go(other, other, yl)]
    mates.append(cp.go(other, other, mate))

    a1[0].wait_recv()
    for zz in range(2):
        def put(at, n, total, zz=zz):
            part[x_right, zz, pl.ds(at, n), :] = total.astype(BF)
        add_rows(put, [lambda at, n, zz=zz: part[x_right, zz, pl.ds(at, n), :], lambda at, n, zz=zz: ra1[0, zz, pl.ds(at, n), :]], half_a)
    a2.append(cp.go(part.at[x_right, :, up_a, :], ra2.at[0, :, up_a, :], xr))
    a1[1].wait_recv()
    for zz in range(2):
        def put(at, n, total, zz=zz):
            part[x_left, zz, pl.ds(half_a + at, n), :] = total.astype(BF)
        add_rows(put, [lambda at, n, zz=zz: part[x_left, zz, pl.ds(half_a + at, n), :], lambda at, n, zz=zz: ra1[1, zz, pl.ds(at, n), :]], half_a)
    a2.append(cp.go(part.at[x_left, :, lo_a, :], ra2.at[1, :, lo_a, :], xl))

    half_k = ROWS // 2
    early, late = pl.ds(0, half_k), pl.ds(half_k, half_k)

    def pass_on(got, zz):
        from_left, from_right = slot(y_left, zz, core), slot(y_right, zz, core)
        got[0].wait_recv()
        first = kv_ref.at[from_left, :, early, :]
        forwards = [cp.go(first, first, yr)]
        got[1].wait_recv()
        second = kv_ref.at[from_right, :, late, :]
        forwards.append(cp.go(second, second, yl))
        for s in (from_left, from_right):
            mates.append(cp.go(kv_ref.at[s], kv_ref.at[s], mate))
        return forwards

    far0 = pass_on(kv_y0, zh)

    bz.wait_recv()

    @pl.loop(0, 4)
    def _(xx):
        part[xx, zl, all_b, :] = (part[xx, zl, all_b, :].astype(F32) + rbz[xx].astype(F32)).astype(BF)

    b1 = [
        cp.go(part.at[x_far, zl, up_b, :], rb1.at[0], xr),
        cp.go(part.at[x_far, zl, lo_b, :], rb1.at[1], xl),
    ]
    b2 = [
        cp.go(part.at[x_right, zl, lo_b, :], rb2.at[0, pl.ds(half_b, half_b), :], xr),
        cp.go(part.at[x_left, zl, up_b, :], rb2.at[1, pl.ds(0, half_b), :], xl),
    ]
    far1 = pass_on(kv_y1, 1 - zh)
    b1[0].wait_recv()
    part[x_right, zl, up_b, :] = (part[x_right, zl, up_b, :].astype(F32) + rb1[0].astype(F32)).astype(BF)
    b2.append(cp.go(part.at[x_right, zl, up_b, :], rb2.at[0, pl.ds(0, half_b), :], xr))
    b1[1].wait_recv()
    part[x_left, zl, lo_b, :] = (part[x_left, zl, lo_b, :].astype(F32) + rb1[1].astype(F32)).astype(BF)
    b2.append(cp.go(part.at[x_left, zl, lo_b, :], rb2.at[1, pl.ds(half_b, half_b), :], xl))

    for copy in a2:
        copy.wait_recv()

    def put_away(at, n, total):
        tz[pl.ds(at, n), :] = total.astype(BF)

    def three(zz):
        return [
            lambda at, n: part[x, zz, pl.ds(at, n), :],
            lambda at, n: ra2[0, zz, pl.ds(at, n), :],
            lambda at, n: ra2[1, zz, pl.ds(at, n), :],
        ]

    add_rows(put_away, three(1 - zl), FIRST)
    az = cp.go(tz, raz, zp)

    for copies, zz in ((far0, zh), (far1, 1 - zh)):
        for copy in copies:
            copy.wait_recv()
        far = kv_ref.at[slot(y_far, zz, core)]
        mates.append(cp.go(far, far, mate))

    deal_do = deal_out(do_own, doz_ref, (dsend, drecv), where)
    for copy in b2:
        copy.wait_recv()

    def put_b(at, n, total):
        do_own[pl.ds(FIRST + at, n), :] = total.astype(BF)

    add_rows(
        put_b,
        [
            lambda at, n: part[x, zl, pl.ds(FIRST + at, n), :],
            lambda at, n: rb2[0, pl.ds(at, n), :],
            lambda at, n: rb2[1, pl.ds(at, n), :],
        ],
        ROWS - FIRST,
    )
    deal_start(deal_do, 3, where)

    def turn(s):
        cols = pl.ds(pl.multiple_of(s * ROWS, ROWS), ROWS)
        kt_ref[:, cols] = kv_ref[s, 0].T
        vt_ref[:, cols] = kv_ref[s, 1].T

    @pl.loop(0, 8)
    def _(i):
        turn(i * 2 + core)

    az.wait_recv()

    def put_a(at, n, total):
        do_own[pl.ds(at, n), :] = total.astype(BF)

    add_rows(put_a, three(zl) + [lambda at, n: raz[pl.ds(at, n), :]], FIRST)
    for r in range(3):
        deal_start(deal_do, r, where)
    deal_keep(do_own, doz_ref, where)

    for copy in mates:
        copy.wait_recv()

    @pl.loop(0, 8)
    def _(i):
        turn(i * 2 + 1 - core)

    deal_wait(q_ref, qz_ref, (qsend, qrecv), where)
    deal_wait(do_own, doz_ref, (dsend, drecv), where)
    cp.finish_sends()


def attend_kernel(
    len_ref, q_ref, do_ref, kv_ref, kt_ref, vt_ref,
    o_ref, dq_ref, dkv_ref,
    qt, qn, dot, don, ot, dqt, acc,
):
    y, zh, core, zl, x = coords()
    starts, run = [], jnp.int32(0)
    for d in range(len_ref.shape[0]):
        starts.append(run)
        run = run + len_ref[d]

    def start_of(pos):
        found = jnp.zeros_like(pos)
        for s in starts:
            found = jnp.maximum(found, jnp.where(s <= pos, s, 0))
        return found

    @pl.loop(0, CTX)
    def _(j):
        acc[j] = jnp.zeros(acc.shape[1:], F32)

    @pl.loop(0, 4)
    def _(slot):
        odd = lax.rem(slot, 2)
        piece = y + odd * (3 - 2 * y)
        seat = zh * 2 + core + odd * (1 - 2 * core)
        row0 = (slot * 16 + seat * 4 + piece) * CHUNK
        rows = pl.ds(pl.multiple_of(slot * CHUNK, CHUNK), CHUNK)
        for h in range(GROUP):
            cols = slice(h * HD, (h + 1) * HD)
            span = slice(h * CHUNK, (h + 1) * CHUNK)
            block = q_ref[rows, cols]
            qn[span, :] = block
            qt[:, span] = block.T
            block = do_ref[rows, cols]
            don[span, :] = block
            dot[:, span] = block.T
        pos = row0 + lax.rem(lax.broadcasted_iota(jnp.int32, (1, GROUP * CHUNK), 1), CHUNK)
        begin = start_of(pos)
        begin_first = start_of(row0)
        begin_last = start_of(row0 + CHUNK - 1)
        low = lax.div(begin_first, ROWS)
        high = lax.div(row0 + CHUNK - 1, ROWS) + 1

        def visible(j):
            key_pos = j * ROWS + lax.broadcasted_iota(jnp.int32, (ROWS, GROUP * CHUNK), 0)
            return jnp.logical_and(key_pos <= pos, key_pos >= begin)

        def whole(j):
            return jnp.logical_and(j * ROWS >= begin_last, (j + 1) * ROWS - 1 <= row0)

        ot[...] = jnp.zeros_like(ot)
        dqt[...] = jnp.zeros_like(dqt)

        def forward(j, carry):
            def step(masked, m, total):
                s = jnp.dot(kv_ref[j, 0], qt[...], preferred_element_type=F32)
                if masked:
                    seen = visible(j)
                    s = jnp.where(seen, s, LOWEST)
                m_new = jnp.maximum(m, jnp.max(s, axis=0, keepdims=True))
                p = jnp.exp2((s - m_new) * TO_LOG2)
                if masked:
                    p = jnp.where(seen, p, 0.0)
                scale = jnp.exp2((m - m_new) * TO_LOG2)
                total = total * scale + jnp.sum(p, axis=0, keepdims=True)
                cols = pl.ds(pl.multiple_of(j * ROWS, ROWS), ROWS)
                ot[...] = ot[...] * scale + jnp.dot(vt_ref[:, cols], p.astype(BF), preferred_element_type=F32)
                return m_new, total

            return lax.cond(whole(j), lambda a, b: step(False, a, b), lambda a, b: step(True, a, b), *carry)

        width = (1, GROUP * CHUNK)
        m, total = lax.fori_loop(low, high, forward, (jnp.full(width, LOWEST, F32), jnp.zeros(width, F32)))
        out = (ot[...] / total).astype(BF)
        delta = jnp.sum(out.astype(F32) * dot[...].astype(F32), axis=0, keepdims=True)
        log_total = m * TO_LOG2 + jnp.log2(total)
        for h in range(GROUP):
            o_ref[rows, slice(h * HD, (h + 1) * HD)] = out[:, h * CHUNK:(h + 1) * CHUNK].T

        def backward(j, carry):
            def step(masked):
                s = jnp.dot(kv_ref[j, 0], qt[...], preferred_element_type=F32)
                dp = jnp.dot(kv_ref[j, 1], dot[...], preferred_element_type=F32)
                if masked:
                    s = jnp.where(visible(j), s, LOWEST)
                p = jnp.exp2(s * TO_LOG2 - log_total)
                ds = (p * (dp - delta)).astype(BF)
                acc[j, 1] += jnp.dot(p.astype(BF), don[...], preferred_element_type=F32)
                acc[j, 0] += jnp.dot(ds, qn[...], preferred_element_type=F32)
                cols = pl.ds(pl.multiple_of(j * ROWS, ROWS), ROWS)
                dqt[...] += jnp.dot(kt_ref[:, cols], ds, preferred_element_type=F32)

            lax.cond(whole(j), lambda: step(False), lambda: step(True))
            return carry

        lax.fori_loop(low, high, backward, 0)
        grads = (dqt[...] * INV_ROOT).astype(BF)
        for h in range(GROUP):
            dq_ref[rows, slice(h * HD, (h + 1) * HD)] = grads[:, h * CHUNK:(h + 1) * CHUNK].T

    @pl.loop(0, CTX)
    def _(j):
        dkv_ref[j, 0] = (acc[j, 0] * INV_ROOT).astype(BF)
        dkv_ref[j, 1] = acc[j, 1].astype(BF)


def return_kernel(
    oz_ref, dqz_ref, dkv_ref, w_ref,
    pr_ref, dq_ref, dk_ref, dv_ref,
    every, total, projz, rc, dsum, r1, r2, tz, rz,
    send, recv, qsend, qrecv, psend, precv,
):
    where = coords()
    y, zh, core, zl, x = where
    greet(*where)
    cp = Copies(send, recv)
    xr, xl = device(y, zh, core, zl, around(x + 1)), device(y, zh, core, zl, around(x - 1))
    zp = device(y, zh, core, 1 - zl, x)
    yr, yl = device(around(y + 1), zh, core, zl, x), device(around(y - 1), zh, core, zl, x)
    hp = device(y, 1 - zh, core, zl, x)
    mate = device(y, zh, 1 - core, zl, x)
    x_right, x_left, x_far = around(x + 1), around(x - 1), around(x + 2)
    y_right, y_left, y_far = around(y + 1), around(y - 1), around(y + 2)
    half_a, half_b = FIRST // 2, (ROWS - FIRST) // 2
    all_a, all_b = pl.ds(0, FIRST), pl.ds(FIRST, 2 * half_b)
    up_a, lo_a = pl.ds(0, half_a), pl.ds(half_a, half_a)
    up_b, lo_b = pl.ds(FIRST, half_b), pl.ds(FIRST + half_b, half_b)

    def same(ref_at, dev):
        return cp.go(ref_at, ref_at, dev)

    core_swap = cp.go(dkv_ref.at[:, 1 - core], rc, mate)
    every[x, zl] = oz_ref[...]
    za = same(every.at[x, zl, all_a, :], zp)
    b0 = [same(every.at[x, zl, all_b, :], xr), same(every.at[x, zl, all_b, :], xl)]
    a0 = [same(every.at[x, zl, all_a, :], xr), same(every.at[x, zl, all_a, :], xl)]

    def deal_back(src, dst, sems, slot):
        yy, zz, cc, r = source_of(slot, y, zh, core)
        return pltpu.make_async_remote_copy(
            src_ref=src.at[pl.ds(slot * CHUNK, CHUNK), :],
            dst_ref=dst.at[pl.ds(r * CHUNK, CHUNK), :],
            send_sem=sems[0].at[slot],
            recv_sem=sems[1].at[r],
            device_id=device(yy, zz, cc, zl, x),
            device_id_type=MESH,
        )

    def start_back(src, dst, sems, slot):
        copy = deal_back(src, dst, sems, slot)
        if slot % 2:
            copy.start()
        else:
            @pl.when(y != slot)
            def _():
                copy.start()

    for s in range(4):
        start_back(dqz_ref, dq_ref, (qsend, qrecv), s)
    deal_keep(dqz_ref, dq_ref, where)

    def times(xx, zz, rows, n):
        at = pl.ds(pl.multiple_of((zz * 4 + xx) * ROWS, ROWS), ROWS)
        total[rows, :] += jnp.dot(every[xx, zz, rows, :], w_ref[at, :], preferred_element_type=F32)

    total[...] = jnp.zeros_like(total)
    times(x, zl, pl.ds(0, ROWS), ROWS)

    core_swap.wait_recv()

    @pl.loop(0, 8)
    def _(b):
        for kind in range(2):
            dsum[b, kind] = (dkv_ref[b, core, kind].astype(F32) + rc[b, kind].astype(F32)).astype(BF)

    half_k = ROWS // 2
    early, late = pl.ds(0, half_k), pl.ds(half_k, half_k)

    def pair(yy):
        return pl.ds(yy * 2, 2)

    d1 = [
        cp.go(dsum.at[pair(y_far), :, early, :], r1.at[0], yr),
        cp.go(dsum.at[pair(y_far), :, late, :], r1.at[1], yl),
    ]
    d2 = [
        cp.go(dsum.at[pair(y_right), :, late, :], r2.at[0, :, :, late, :], yr),
        cp.go(dsum.at[pair(y_left), :, early, :], r2.at[1, :, :, early, :], yl),
    ]

    za.wait_recv()
    a1 = [same(every.at[x, 1 - zl, all_a, :], xr), same(every.at[x, 1 - zl, all_a, :], xl)]
    times(x, 1 - zl, all_a, FIRST)

    b0[0].wait_recv()
    fb = [same(every.at[x_left, zl, up_b, :], xr)]
    b0[1].wait_recv()
    fb.append(same(every.at[x_right, zl, lo_b, :], xl))
    a0[0].wait_recv()
    fa0 = [same(every.at[x_left, zl, up_a, :], xr)]
    a0[1].wait_recv()
    fa0.append(same(every.at[x_right, zl, lo_a, :], xl))
    times(x_left, zl, pl.ds(0, ROWS), ROWS)
    times(x_right, zl, pl.ds(0, ROWS), ROWS)

    d1[0].wait_recv()

    def add_into(zz, kind, which, yy, rows):
        dsum[yy * 2 + zz, kind, rows, :] = (
            dsum[yy * 2 + zz, kind, rows, :].astype(F32) + r1[which, zz, kind].astype(F32)
        ).astype(BF)

    for zz in range(2):
        for kind in range(2):
            add_into(zz, kind, 0, y_right, early)
    d2.append(cp.go(dsum.at[pair(y_right), :, early, :], r2.at[0, :, :, early, :], yr))
    d1[1].wait_recv()
    for zz in range(2):
        for kind in range(2):
            add_into(zz, kind, 1, y_left, late)
    d2.append(cp.go(dsum.at[pair(y_left), :, late, :], r2.at[1, :, :, late, :], yl))

    for copy in fb:
        copy.wait_recv()
    zb = same(every.at[:, zl, all_b, :], zp)

    a1[0].wait_recv()
    fa1 = [same(every.at[x_left, 1 - zl, up_a, :], xr)]
    a1[1].wait_recv()
    fa1.append(same(every.at[x_right, 1 - zl, lo_a, :], xl))
    times(x_left, 1 - zl, all_a, FIRST)
    times(x_right, 1 - zl, all_a, FIRST)
    for copy in fa0:
        copy.wait_recv()
    times(x_far, zl, pl.ds(0, ROWS), ROWS)

    for copy in d2:
        copy.wait_recv()

    def three(zz, kind):
        return (
            dsum[y * 2 + zz, kind].astype(F32)
            + r2[0, zz, kind].astype(F32)
            + r2[1, zz, kind].astype(F32)
        )

    for kind in range(2):
        tz[kind] = three(1 - zh, kind).astype(BF)
    dz = cp.go(tz, rz, hp)

    for copy in fa1:
        copy.wait_recv()
    times(x_far, 1 - zl, all_a, FIRST)
    zb.wait_recv()

    @pl.loop(0, 4)
    def _(xx):
        times(xx, 1 - zl, all_b, ROWS - FIRST)

    projz[...] = total[...].astype(BF)
    for s in range(4):
        start_back(projz, pr_ref, (psend, precv), s)
    deal_keep(projz, pr_ref, where)

    dz.wait_recv()
    dk_ref[...] = (three(zh, 0) + rz[0].astype(F32)).astype(BF)
    dv_ref[...] = (three(zh, 1) + rz[1].astype(F32)).astype(BF)

    deal_wait(dqz_ref, dq_ref, (qsend, qrecv), where)
    deal_wait(projz, pr_ref, (psend, precv), where)
    cp.finish_sends()


def shape(*dims, dtype=BF):
    return jax.ShapeDtypeStruct(dims, dtype)


def params(collective=None):
    if collective is None:
        return pltpu.CompilerParams(vmem_limit_bytes=56 << 20)
    return pltpu.CompilerParams(
        collective_id=collective, has_side_effects=True, vmem_limit_bytes=56 << 20
    )


IN_VMEM = pl.BlockSpec(memory_space=pltpu.VMEM)
IN_SMEM = pl.BlockSpec(memory_space=pltpu.SMEM)
DMA = pltpu.SemaphoreType.DMA


def gather(queries, key_input, value_input, grad_projected, out_weight):
    half_a, half_b = FIRST // 2, (ROWS - FIRST) // 2
    return pl.pallas_call(
        gather_kernel,
        out_shape=(
            shape(ROWS, ROWS),
            shape(CTX, 2, ROWS, HD),
            shape(HD, TOKENS),
            shape(HD, TOKENS),
            shape(ROWS, ROWS),
        ),
        in_specs=[IN_VMEM] * 5,
        out_specs=(IN_VMEM,) * 5,
        scratch_shapes=[
            pltpu.VMEM((4, 2, ROWS, ROWS), BF),
            pltpu.VMEM((2, 2, half_a, ROWS), BF),
            pltpu.VMEM((2, 2, FIRST, ROWS), BF),
            pltpu.VMEM((FIRST, ROWS), BF),
            pltpu.VMEM((FIRST, ROWS), BF),
            pltpu.VMEM((4, ROWS - FIRST, ROWS), BF),
            pltpu.VMEM((2, half_b, ROWS), BF),
            pltpu.VMEM((2, ROWS - FIRST, ROWS), BF),
            pltpu.VMEM((ROWS, ROWS), BF),
            DMA((40,)), DMA((40,)),
            DMA((4,)), DMA((4,)), DMA((4,)), DMA((4,)),
        ],
        compiler_params=params(0),
        name="gather_inputs",
    )(queries, key_input, value_input, grad_projected, out_weight)


def attend(lengths, queries, grads, kv, keys_t, values_t):
    wide = GROUP * CHUNK
    return pl.pallas_call(
        attend_kernel,
        out_shape=(shape(ROWS, ROWS), shape(ROWS, ROWS), shape(CTX, 2, ROWS, HD)),
        in_specs=[IN_SMEM] + [IN_VMEM] * 5,
        out_specs=(IN_VMEM,) * 3,
        scratch_shapes=[
            pltpu.VMEM((HD, wide), BF),
            pltpu.VMEM((wide, HD), BF),
            pltpu.VMEM((HD, wide), BF),
            pltpu.VMEM((wide, HD), BF),
            pltpu.VMEM((HD, wide), F32),
            pltpu.VMEM((HD, wide), F32),
            pltpu.VMEM((CTX, 2, ROWS, HD), F32),
        ],
        compiler_params=params(),
        name="attend",
    )(lengths, queries, grads, kv, keys_t, values_t)


def give_back(attention, query_grads, kv_grads, out_weight):
    return pl.pallas_call(
        return_kernel,
        out_shape=(shape(ROWS, ROWS), shape(ROWS, ROWS), shape(ROWS, HD), shape(ROWS, HD)),
        in_specs=[IN_VMEM] * 4,
        out_specs=(IN_VMEM,) * 4,
        scratch_shapes=[
            pltpu.VMEM((4, 2, ROWS, ROWS), BF),
            pltpu.VMEM((ROWS, ROWS), F32),
            pltpu.VMEM((ROWS, ROWS), BF),
            pltpu.VMEM((8, 2, ROWS, HD), BF),
            pltpu.VMEM((8, 2, ROWS, HD), BF),
            pltpu.VMEM((2, 2, 2, ROWS // 2, HD), BF),
            pltpu.VMEM((2, 2, 2, ROWS, HD), BF),
            pltpu.VMEM((2, ROWS, HD), BF),
            pltpu.VMEM((2, ROWS, HD), BF),
            DMA((40,)), DMA((40,)),
            DMA((4,)), DMA((4,)), DMA((4,)), DMA((4,)),
        ],
        compiler_params=params(1),
        name="give_back",
    )(attention, query_grads, kv_grads.reshape(8, 2, 2, ROWS, HD), out_weight)


def body(queries, key_input, value_input, out_weight, lengths, grad_projected):
    qz, kv, keys_t, values_t, gz = gather(
        queries, key_input, value_input, grad_projected, out_weight
    )
    attention, dq, dkv = attend(lengths, qz, gz, kv, keys_t, values_t)
    return give_back(attention, dq, dkv, out_weight)


def solution(mesh):
    both = P("ctx", "head")
    return jax.shard_map(
        body,
        mesh=mesh,
        in_specs=(both, both, both, P(None, "head"), P(), both),
        out_specs=(both, both, both, both),
        check_vma=False,
    )
```

time: 731 us -> 175 us (0.24)
  the two profiles are of different devices: /device:TPU:25 before, /device:TPU:1 now
where the time goes in v1:
time: 175 us; the launch traced here: 174 us
  Pallas kernels  167 us (95%)
  local copies, waits for them, and re-layouts  6.87 us (4%)
    pallas_call x1, Pallas kernels, gather(): pl.pallas_call(gather_kernel, out_shape=(shape(ROWS, ROWS), shape(CTX, 2,...  59 us
    pallas_call x1, Pallas kernels, give_back(): pl.pallas_call(return_kernel, out_shape=(shape(ROWS, ROWS), shape(ROWS, R...  57 us
    pallas_call x1, Pallas kernels, attend(): pl.pallas_call(attend_kernel, out_shape=(shape(ROWS, ROWS), shape(ROWS, R...  50.7 us
    unnamed x4, local copies, waits for them, and re-layouts  6.87 us

profile of v1, /device:TPU:1, one launch (start us, length us, event | category | flops | bytes accessed | tf_op | source)
XLA Modules:
  0.0 174.2 jit_solution(6232311327363801867)
XLA Ops:
  0.6 59.0 %gather_inputs.1 = (bf16[512,512]{1,0:T(8,128)(2,1)}, bf16[16,2,512,128]{3,2,1,0:T(8,128)(2,1)}, bf16[128,8192]{1,0:T(8,128)(2,1)}, bf16[128,8192]{1,0:T(8,128)(2,1)}, bf16[512,512]{1,0:T(8,128)(2,1)}) custom-call(bf16[512,512]{1,0:T(8,128)(2,1)} %q_ref.1, bf16[512,128]{1,0:T(8,128)(2,1)} %k_ref.1, bf16[512,128]{1,0:T(8,128)(2,1)} %v_ref.1, ...), custom_call_target="tpu_custom_call" | custom-call | tf_op jit(solution)/shard_map/gather_inputs/pallas_call | solution.py:638
  59.6 50.7 %attend.1 = (bf16[512,512]{1,0:T(8,128)(2,1)}, bf16[512,512]{1,0:T(8,128)(2,1)}, bf16[16,2,512,128]{3,2,1,0:T(8,128)(2,1)}) custom-call(s32[6]{0:T(128)} %len_ref.1, bf16[512,512]{1,0:T(8,128)(2,1)} %get-tuple-element.12.q_ref, bf16[512,512]{1,0:T(8,128)(2,1)} %get-tuple-element.13.do_ref, bf16[16,2,512,128]{3,2,1,0:T(8,128)(2,1)} %get-tuple-element.14.kv_ref, ...), custom_call_target="tpu_custom_call" | custom-call | tf_op jit(solution)/shard_map/attend/pallas_call | solution.py:669
  110.3 57.0 %give_back.1 = (bf16[512,512]{1,0:T(8,128)(2,1)}, bf16[512,512]{1,0:T(8,128)(2,1)}, bf16[512,128]{1,0:T(8,128)(2,1)}, bf16[512,128]{1,0:T(8,128)(2,1)}) custom-call(bf16[512,512]{1,0:T(8,128)(2,1)} %get-tuple-element.17.oz_ref, bf16[512,512]{1,0:T(8,128)(2,1)} %get-tuple-element.18.dqz_ref, bf16[8,2,2,512,128]{4,3,2,1,0:T(8,128)(2,1)} %bitcast.1, ...), custom_call_target="tpu_custom_call" | custom-call | tf_op jit(solution)/shard_map/give_back/pallas_call | solution.py:689
  167.3 1.9 %copy.14 = bf16[512,512]{1,0:T(8,128)(2,1)} copy(bf16[512,512]{1,0:T(8,128)(2,1)} %get-tuple-element.24) | data formatting | bytes 1048576
  169.2 1.9 %copy.15 = bf16[512,512]{1,0:T(8,128)(2,1)} copy(bf16[512,512]{1,0:T(8,128)(2,1)} %get-tuple-element.25) | data formatting | bytes 1048576
  171.0 1.6 copy.16
  172.6 1.6 copy.17

commit v2 on v1

v2 whole, which is shorter than its diff:
```python
import math

import jax
import jax.numpy as jnp
from jax import lax
from jax.experimental import pallas as pl
from jax.experimental.pallas import tpu as pltpu
from jax.sharding import PartitionSpec as P

HD = 128
GROUP = 4
ROWS = 512
CHUNK = 128
CTX = 16
TOKENS = 8192
INV_ROOT = 1.0 / math.sqrt(HD)
TO_LOG2 = INV_ROOT * math.log2(math.e)
LOWEST = -1e30
FLIP_Z = 0
FIRST = 384
MESH = pl.DeviceIdType.MESH
BF = jnp.bfloat16
F32 = jnp.float32


def coords():
    c = lax.axis_index("ctx")
    h = lax.axis_index("head")
    y = lax.div(c, 4)
    zh = lax.rem(lax.div(c, 2), 2)
    core = lax.rem(c, 2)
    zl = lax.div(h, 4)
    x = lax.rem(h, 4)
    return y, zh, core, zl, x


def device(y, zh, core, zl, x):
    return {"ctx": y * 4 + zh * 2 + core, "head": zl * 4 + x}


def around(i):
    return lax.rem(i + 4, 4)


def source_of(slot, y, zh, core):
    if slot % 2 == 0:
        return slot, zh, core, y
    return slot, zh + FLIP_Z * (1 - 2 * zh), 1 - core, 3 - y


class Copies:
    def __init__(self, send, recv):
        self.send, self.recv = send, recv
        self.made = []
        self.next = 0

    def new(self, src, dst, dev):
        i = self.next
        self.next += 1
        copy = pltpu.make_async_remote_copy(
            src_ref=src,
            dst_ref=dst,
            send_sem=self.send.at[i],
            recv_sem=self.recv.at[i],
            device_id=dev,
            device_id_type=MESH,
        )
        self.made.append(copy)
        return copy

    def go(self, src, dst, dev):
        copy = self.new(src, dst, dev)
        copy.start()
        return copy

    def finish_sends(self):
        for copy in self.made:
            copy.wait_send()


def greet(y, zh, core, zl, x):
    barrier = pltpu.get_barrier_semaphore()
    c = y * 4 + zh * 2 + core
    peers = [device(y, zh, core, zl, around(x + 1)), device(y, zh, core, zl, around(x - 1)), device(y, zh, core, 1 - zl, x)]
    for step in range(1, CTX):
        peers.append({"ctx": lax.rem(c + step, CTX), "head": zl * 4 + x})
    for peer in peers:
        pl.semaphore_signal(barrier, inc=1, device_id=peer, device_id_type=MESH)
    pl.semaphore_wait(barrier, len(peers))


def deal_out(src, dst, sems, where):
    y, zh, core, zl, x = where
    send, recv = sems
    odd = lax.rem(y, 2)
    copies = []
    for r in range(4):
        copy = pltpu.make_async_remote_copy(
            src_ref=src.at[pl.ds(r * CHUNK, CHUNK), :],
            dst_ref=dst.at[pl.ds(y * CHUNK, CHUNK), :],
            send_sem=send.at[r],
            recv_sem=recv.at[y],
            device_id=device(
                r + odd * (3 - 2 * r), zh + odd * FLIP_Z * (1 - 2 * zh), core + odd * (1 - 2 * core), zl, x
            ),
            device_id_type=MESH,
        )
        copies.append(copy)
    return copies


def deal_start(copies, r, where):
    y = where[0]
    mine = jnp.logical_and(lax.rem(y, 2) == 0, y == r)

    @pl.when(jnp.logical_not(mine))
    def _():
        copies[r].start()


def deal_keep(src, dst, where):
    y = where[0]

    @pl.when(lax.rem(y, 2) == 0)
    def _():
        rows = pl.ds(y * CHUNK, CHUNK)
        dst[rows, :] = src[rows, :]


def deal_wait(src, dst, sems, where):
    y, zh, core, zl, x = where
    send, recv = sems
    for r in range(4):
        for kind in (0, 1):
            mine = jnp.logical_and(lax.rem(y, 2) == 0, y == r)

            @pl.when(jnp.logical_not(mine))
            def _():
                copy = pltpu.make_async_remote_copy(
                    src_ref=src.at[pl.ds(r * CHUNK, CHUNK), :],
                    dst_ref=dst.at[pl.ds(r * CHUNK, CHUNK), :],
                    send_sem=send.at[r],
                    recv_sem=recv.at[r],
                    device_id=device(y, zh, 1 - core, zl, x),
                    device_id_type=MESH,
                )
                if kind == 0:
                    copy.wait_recv()
                else:
                    copy.wait_send()


def add_rows(dst_at, parts, rows, step=64):
    @pl.loop(0, rows // step)
    def _(i):
        at = pl.multiple_of(i * step, step)
        total = parts[0](at, step).astype(F32)
        for part in parts[1:]:
            total = total + part(at, step).astype(F32)
        dst_at(at, step, total)


def layer_kernel(
    len_ref, q_ref, k_ref, v_ref, gp_ref, w_ref,
    pr_ref, dq_ref, dk_ref, dv_ref,
    qz_ref, kv_ref, kt_ref, vt_ref, doz_ref, oz_ref, dqz_ref,
    part, ra1, ra2, raz, tz, rbz, rb1, rb2, do_own,
    qt, qn, dot, don, ot, outs, logs, deltas, dqt, acc,
    every, total, projz, dkv_out, rc, dsum, r1, r2, tzk, rz,
    send, recv, qsend, qrecv, dsend, drecv, gsend, grecv, psend, precv,
):
    where = coords()
    y, zh, core, zl, x = where
    c = y * 4 + zh * 2 + core
    greet(*where)
    cp = Copies(send, recv)
    xr, xl = device(y, zh, core, zl, around(x + 1)), device(y, zh, core, zl, around(x - 1))
    zp = device(y, zh, core, 1 - zl, x)
    yr, yl = device(around(y + 1), zh, core, zl, x), device(around(y - 1), zh, core, zl, x)
    hp = device(y, 1 - zh, core, zl, x)
    mate = device(y, zh, 1 - core, zl, x)
    x_right, x_left, x_far = around(x + 1), around(x - 1), around(x + 2)
    y_right, y_left, y_far = around(y + 1), around(y - 1), around(y + 2)
    half_a, half_b = FIRST // 2, (ROWS - FIRST) // 2

    def slot(yy, zz, cc):
        return yy * 4 + zz * 2 + cc

    kv_ref[c, 0] = k_ref[...]
    kv_ref[c, 1] = v_ref[...]
    own = kv_ref.at[c]
    kv_z = cp.go(own, own, hp)
    kv_y0 = [cp.go(own, own, yr), cp.go(own, own, yl)]
    mates = [cp.go(own, own, mate)]
    deal_q = deal_out(q_ref, qz_ref, (qsend, qrecv), where)

    for r in range(4):
        deal_start(deal_q, r, where)
    deal_keep(q_ref, qz_ref, where)

    def compute(xx):
        @pl.loop(0, 2)
        def _(zz):
            rows = pl.ds(pl.multiple_of((zz * 4 + xx) * ROWS, ROWS), ROWS)
            part[xx, zz] = lax.dot_general(
                gp_ref[...], w_ref[rows, :], (((1,), (1,)), ((), ())), preferred_element_type=F32
            ).astype(BF)

    up_a, lo_a = pl.ds(0, half_a), pl.ds(half_a, half_a)
    all_b = pl.ds(FIRST, 2 * half_b)
    up_b, lo_b = pl.ds(FIRST, half_b), pl.ds(FIRST + half_b, half_b)
    compute(x_far)
    a1 = [
        cp.go(part.at[x_far, :, up_a, :], ra1.at[0], xr),
        cp.go(part.at[x_far, :, lo_a, :], ra1.at[1], xl),
    ]
    compute(x_right)
    a2 = [cp.go(part.at[x_right, :, lo_a, :], ra2.at[0, :, lo_a, :], xr)]
    compute(x_left)
    a2.append(cp.go(part.at[x_left, :, up_a, :], ra2.at[1, :, up_a, :], xl))
    compute(x)
    bz = cp.go(part.at[:, 1 - zl, all_b, :], rbz, zp)

    kv_z.wait_recv()
    other = kv_ref.at[slot(y, 1 - zh, core)]
    kv_y1 = [cp.go(other, other, yr), cp.go(other, other, yl)]
    mates.append(cp.go(other, other, mate))

    a1[0].wait_recv()
    for zz in range(2):
        def put(at, n, total, zz=zz):
            part[x_right, zz, pl.ds(at, n), :] = total.astype(BF)
        add_rows(put, [lambda at, n, zz=zz: part[x_right, zz, pl.ds(at, n), :], lambda at, n, zz=zz: ra1[0, zz, pl.ds(at, n), :]], half_a)
    a2.append(cp.go(part.at[x_right, :, up_a, :], ra2.at[0, :, up_a, :], xr))
    a1[1].wait_recv()
    for zz in range(2):
        def put(at, n, total, zz=zz):
            part[x_left, zz, pl.ds(half_a + at, n), :] = total.astype(BF)
        add_rows(put, [lambda at, n, zz=zz: part[x_left, zz, pl.ds(half_a + at, n), :], lambda at, n, zz=zz: ra1[1, zz, pl.ds(at, n), :]], half_a)
    a2.append(cp.go(part.at[x_left, :, lo_a, :], ra2.at[1, :, lo_a, :], xl))

    half_k = ROWS // 2
    early, late = pl.ds(0, half_k), pl.ds(half_k, half_k)

    def pass_on(got, zz):
        from_left, from_right = slot(y_left, zz, core), slot(y_right, zz, core)
        got[0].wait_recv()
        first = kv_ref.at[from_left, :, early, :]
        forwards = [cp.go(first, first, yr)]
        got[1].wait_recv()
        second = kv_ref.at[from_right, :, late, :]
        forwards.append(cp.go(second, second, yl))
        for s in (from_left, from_right):
            mates.append(cp.go(kv_ref.at[s], kv_ref.at[s], mate))
        return forwards

    far0 = pass_on(kv_y0, zh)

    bz.wait_recv()

    @pl.loop(0, 4)
    def _(xx):
        part[xx, zl, all_b, :] = (part[xx, zl, all_b, :].astype(F32) + rbz[xx].astype(F32)).astype(BF)

    b1 = [
        cp.go(part.at[x_far, zl, up_b, :], rb1.at[0], xr),
        cp.go(part.at[x_far, zl, lo_b, :], rb1.at[1], xl),
    ]
    b2 = [
        cp.go(part.at[x_right, zl, lo_b, :], rb2.at[0, pl.ds(half_b, half_b), :], xr),
        cp.go(part.at[x_left, zl, up_b, :], rb2.at[1, pl.ds(0, half_b), :], xl),
    ]
    far1 = pass_on(kv_y1, 1 - zh)
    for copies, zz in ((far0, zh), (far1, 1 - zh)):
        for copy in copies:
            copy.wait_recv()
        far = kv_ref.at[slot(y_far, zz, core)]
        mates.append(cp.go(far, far, mate))

    def turn(s):
        cols = pl.ds(pl.multiple_of(s * ROWS, ROWS), ROWS)
        kt_ref[:, cols] = kv_ref[s, 0].T
        vt_ref[:, cols] = kv_ref[s, 1].T

    @pl.loop(0, 8)
    def _(i):
        turn(i * 2 + core)

    for copy in mates:
        copy.wait_recv()

    @pl.loop(0, 8)
    def _(i):
        turn(i * 2 + 1 - core)

    deal_wait(q_ref, qz_ref, (qsend, qrecv), where)

    starts, run = [], jnp.int32(0)
    for d in range(len_ref.shape[0]):
        starts.append(run)
        run = run + len_ref[d]
    wide = GROUP * CHUNK

    def place(slot):
        odd = lax.rem(slot, 2)
        piece = y + odd * (3 - 2 * y)
        seat = (zh + odd * FLIP_Z * (1 - 2 * zh)) * 2 + core + odd * (1 - 2 * core)
        return seat, (slot * 16 + seat * 4 + piece) * CHUNK

    def positions(slot):
        row0 = place(slot)[1]
        pos = row0 + lax.rem(lax.broadcasted_iota(jnp.int32, (1, wide), 1), CHUNK)
        begin = jnp.zeros_like(pos)
        for at in starts:
            begin = jnp.maximum(begin, jnp.where(at <= pos, at, 0))
        return pos, begin

    def masked_scores(j, slot, pos, begin):
        s = jnp.dot(kv_ref[j, 0], qt[slot], preferred_element_type=F32)
        key_pos = j * ROWS + lax.broadcasted_iota(jnp.int32, (ROWS, wide), 0)
        seen = jnp.logical_and(key_pos <= pos, key_pos >= begin)
        return jnp.where(seen, s, LOWEST)

    def columns(j):
        return pl.ds(pl.multiple_of(j * ROWS, ROWS), ROWS)

    def attend_slot(slot):
        rows = pl.ds(pl.multiple_of(slot * CHUNK, CHUNK), CHUNK)
        for h in range(GROUP):
            cols = slice(h * HD, (h + 1) * HD)
            span = slice(h * CHUNK, (h + 1) * CHUNK)
            block = qz_ref[rows, cols]
            qn[slot, span, :] = block
            qt[slot, :, span] = block.T
        pos, begin = positions(slot)
        ot[...] = jnp.zeros_like(ot)

        def step(blocks, m, total):
            ss = [masked_scores(j, slot, pos, begin) for j in blocks]
            m_new = m
            for s in ss:
                m_new = jnp.maximum(m_new, jnp.max(s, axis=0, keepdims=True))
            base = jnp.maximum(m_new, 0.5 * LOWEST)
            scale = jnp.exp2((m - base) * TO_LOG2)
            total = total * scale
            kept = ot[...] * scale
            for j, s in zip(blocks, ss):
                p = jnp.exp2((s - base) * TO_LOG2)
                total = total + jnp.sum(p, axis=0, keepdims=True)
                kept = kept + jnp.dot(vt_ref[:, columns(j)], p.astype(BF), preferred_element_type=F32)
            ot[...] = kept
            return m_new, total

        count = 4 * slot + place(slot)[0] + 1
        carry = (jnp.full((1, wide), LOWEST, F32), jnp.zeros((1, wide), F32))
        carry = lax.fori_loop(
            0, lax.div(count, 2), lambda i, c: step((2 * i, 2 * i + 1), *c), carry
        )
        m, total = lax.fori_loop(
            0, lax.rem(count, 2), lambda i, c: step((count - 1,), *c), carry
        )
        out = (ot[...] / total).astype(BF)
        outs[slot] = out
        logs[slot] = m * TO_LOG2 + jnp.log2(total)
        for h in range(GROUP):
            oz_ref[rows, slice(h * HD, (h + 1) * HD)] = out[:, h * CHUNK:(h + 1) * CHUNK].T

    @pl.loop(0, 2)
    def _(slot):
        attend_slot(slot)

    b1[0].wait_recv()
    part[x_right, zl, up_b, :] = (part[x_right, zl, up_b, :].astype(F32) + rb1[0].astype(F32)).astype(BF)
    b2.append(cp.go(part.at[x_right, zl, up_b, :], rb2.at[0, pl.ds(0, half_b), :], xr))
    b1[1].wait_recv()
    part[x_left, zl, lo_b, :] = (part[x_left, zl, lo_b, :].astype(F32) + rb1[1].astype(F32)).astype(BF)
    b2.append(cp.go(part.at[x_left, zl, lo_b, :], rb2.at[1, pl.ds(half_b, half_b), :], xl))

    attend_slot(jnp.int32(2))

    for copy in a2:
        copy.wait_recv()

    def put_away(at, n, total):
        tz[pl.ds(at, n), :] = total.astype(BF)

    def three(zz):
        return [
            lambda at, n: part[x, zz, pl.ds(at, n), :],
            lambda at, n: ra2[0, zz, pl.ds(at, n), :],
            lambda at, n: ra2[1, zz, pl.ds(at, n), :],
        ]

    add_rows(put_away, three(1 - zl), FIRST)
    az = cp.go(tz, raz, zp)

    attend_slot(jnp.int32(3))

    deal_do = deal_out(do_own, doz_ref, (dsend, drecv), where)
    for copy in b2:
        copy.wait_recv()

    def put_b(at, n, total):
        do_own[pl.ds(FIRST + at, n), :] = total.astype(BF)

    add_rows(
        put_b,
        [
            lambda at, n: part[x, zl, pl.ds(FIRST + at, n), :],
            lambda at, n: rb2[0, pl.ds(at, n), :],
            lambda at, n: rb2[1, pl.ds(at, n), :],
        ],
        ROWS - FIRST,
    )
    deal_start(deal_do, 3, where)

    all_a = pl.ds(0, FIRST)
    def same(ref_at, dev):
        return cp.go(ref_at, ref_at, dev)

    every[x, zl] = oz_ref[...]
    za = same(every.at[x, zl, all_a, :], zp)
    b0 = [same(every.at[x, zl, all_b, :], xr), same(every.at[x, zl, all_b, :], xl)]
    a0 = [same(every.at[x, zl, all_a, :], xr), same(every.at[x, zl, all_a, :], xl)]

    az.wait_recv()

    def put_a(at, n, total):
        do_own[pl.ds(at, n), :] = total.astype(BF)

    add_rows(put_a, three(zl) + [lambda at, n: raz[pl.ds(at, n), :]], FIRST)
    for r in range(3):
        deal_start(deal_do, r, where)
    deal_keep(do_own, doz_ref, where)

    def deal_back(src, dst, sems, slot):
        yy, zz, cc, r = source_of(slot, y, zh, core)
        return pltpu.make_async_remote_copy(
            src_ref=src.at[pl.ds(slot * CHUNK, CHUNK), :],
            dst_ref=dst.at[pl.ds(r * CHUNK, CHUNK), :],
            send_sem=sems[0].at[slot],
            recv_sem=sems[1].at[r],
            device_id=device(yy, zz, cc, zl, x),
            device_id_type=MESH,
        )

    def start_back(src, dst, sems, slot):
        copy = deal_back(src, dst, sems, slot)
        if slot % 2:
            copy.start()
        else:
            @pl.when(y != slot)
            def _():
                copy.start()

    def times(xx, zz, rows, n):
        at = pl.ds(pl.multiple_of((zz * 4 + xx) * ROWS, ROWS), ROWS)
        total[rows, :] += jnp.dot(every[xx, zz, rows, :], w_ref[at, :], preferred_element_type=F32)

    total[...] = jnp.zeros_like(total)
    times(x, zl, pl.ds(0, ROWS), ROWS)

    deal_wait(do_own, doz_ref, (dsend, drecv), where)

    @pl.loop(0, 4)
    def _(slot):
        rows = pl.ds(pl.multiple_of(slot * CHUNK, CHUNK), CHUNK)
        for h in range(GROUP):
            cols = slice(h * HD, (h + 1) * HD)
            span = slice(h * CHUNK, (h + 1) * CHUNK)
            block = doz_ref[rows, cols]
            don[slot, span, :] = block
            dot[slot, :, span] = block.T
        deltas[slot] = jnp.sum(outs[slot].astype(F32) * dot[slot].astype(F32), axis=0, keepdims=True)
        dqt[slot] = jnp.zeros(dqt.shape[1:], F32)

    @pl.loop(0, CTX)
    def _(j):
        acc[j] = jnp.zeros(acc.shape[1:], F32)

    half_k = ROWS // 2
    early, late = pl.ds(0, half_k), pl.ds(half_k, half_k)

    def sweep_quarter(yy):
        @pl.loop(yy, 4)
        def _(slot):
            pos, begin = positions(slot)
            log_total, delta = logs[slot], deltas[slot]

            def unit(j):
                s = masked_scores(j, slot, pos, begin)
                dp = jnp.dot(kv_ref[j, 1], dot[slot], preferred_element_type=F32)
                p = jnp.exp2(s * TO_LOG2 - log_total)
                ds = (p * (dp - delta)).astype(BF)
                acc[j, 1] += jnp.dot(p.astype(BF), don[slot], preferred_element_type=F32)
                acc[j, 0] += jnp.dot(ds, qn[slot], preferred_element_type=F32)
                dqt[slot] += jnp.dot(kt_ref[:, columns(j)], ds, preferred_element_type=F32)

            count = jnp.where(slot == yy, place(slot)[0] + 1, 4)

            @pl.loop(0, lax.div(count, 2))
            def _(i):
                unit(4 * yy + 2 * i)
                unit(4 * yy + 2 * i + 1)

            @pl.loop(0, lax.rem(count, 2))
            def _(i):
                unit(4 * yy + count - 1)

        @pl.loop(0, 2)
        def _(zz):
            j = yy * 4 + zz * 2 + 1 - core
            mine = yy * 2 + zz
            dkv_out[mine, 0] = (acc[j, 0] * INV_ROOT).astype(BF)
            dkv_out[mine, 1] = acc[j, 1].astype(BF)

        return cp.go(dkv_out.at[pair(yy)], rc.at[pair(yy)], mate)

    def pair(yy):
        return pl.ds(yy * 2, 2)

    def join(yy, swap):
        swap.wait_recv()

        @pl.loop(0, 2)
        def _(zz):
            j = yy * 4 + zz * 2 + core
            mine = yy * 2 + zz
            dsum[mine, 0] = (acc[j, 0] * INV_ROOT + rc[mine, 0].astype(F32)).astype(BF)
            dsum[mine, 1] = (acc[j, 1] + rc[mine, 1].astype(F32)).astype(BF)

    swap_far = sweep_quarter(y_far)
    za.wait_recv()
    a1 = [same(every.at[x, 1 - zl, all_a, :], xr), same(every.at[x, 1 - zl, all_a, :], xl)]
    b0[0].wait_recv()
    fb = [same(every.at[x_left, zl, up_b, :], xr)]
    b0[1].wait_recv()
    fb.append(same(every.at[x_right, zl, lo_b, :], xl))
    a0[0].wait_recv()
    fa0 = [same(every.at[x_left, zl, up_a, :], xr)]
    a0[1].wait_recv()
    fa0.append(same(every.at[x_right, zl, lo_a, :], xl))
    times(x, 1 - zl, all_a, FIRST)

    swap_right = sweep_quarter(y_right)
    join(y_far, swap_far)
    d1 = [
        cp.go(dsum.at[pair(y_far), :, early, :], r1.at[0], yr),
        cp.go(dsum.at[pair(y_far), :, late, :], r1.at[1], yl),
    ]
    a1[0].wait_recv()
    fa1 = [same(every.at[x_left, 1 - zl, up_a, :], xr)]
    a1[1].wait_recv()
    fa1.append(same(every.at[x_right, 1 - zl, lo_a, :], xl))
    times(x_left, zl, pl.ds(0, ROWS), ROWS)
    times(x_right, zl, pl.ds(0, ROWS), ROWS)

    swap_left = sweep_quarter(y_left)
    join(y_right, swap_right)
    d2 = [cp.go(dsum.at[pair(y_right), :, late, :], r2.at[0, :, :, late, :], yr)]
    for copy in fb:
        copy.wait_recv()
    zb = same(every.at[:, zl, all_b, :], zp)

    times(x_left, 1 - zl, all_a, FIRST)
    times(x_right, 1 - zl, all_a, FIRST)
    swap_own = sweep_quarter(y)

    @pl.loop(0, 4)
    def _(slot):
        rows = pl.ds(pl.multiple_of(slot * CHUNK, CHUNK), CHUNK)
        grads = (dqt[slot] * INV_ROOT).astype(BF)
        for h in range(GROUP):
            dqz_ref[rows, slice(h * HD, (h + 1) * HD)] = grads[:, h * CHUNK:(h + 1) * CHUNK].T

    join(y_left, swap_left)
    d2.append(cp.go(dsum.at[pair(y_left), :, early, :], r2.at[1, :, :, early, :], yl))
    for s in range(4):
        start_back(dqz_ref, dq_ref, (gsend, grecv), s)
    deal_keep(dqz_ref, dq_ref, where)

    d1[0].wait_recv()

    def add_into(zz, kind, which, yy, rows):
        dsum[yy * 2 + zz, kind, rows, :] = (
            dsum[yy * 2 + zz, kind, rows, :].astype(F32) + r1[which, zz, kind].astype(F32)
        ).astype(BF)

    for zz in range(2):
        for kind in range(2):
            add_into(zz, kind, 0, y_right, early)
    d2.append(cp.go(dsum.at[pair(y_right), :, early, :], r2.at[0, :, :, early, :], yr))
    d1[1].wait_recv()
    for zz in range(2):
        for kind in range(2):
            add_into(zz, kind, 1, y_left, late)
    d2.append(cp.go(dsum.at[pair(y_left), :, late, :], r2.at[1, :, :, late, :], yl))

    for copy in fa0:
        copy.wait_recv()
    times(x_far, zl, pl.ds(0, ROWS), ROWS)

    join(y, swap_own)
    for copy in d2:
        copy.wait_recv()

    def three(zz, kind):
        return (
            dsum[y * 2 + zz, kind].astype(F32)
            + r2[0, zz, kind].astype(F32)
            + r2[1, zz, kind].astype(F32)
        )

    for kind in range(2):
        tzk[kind] = three(1 - zh, kind).astype(BF)
    dz = cp.go(tzk, rz, hp)

    for copy in fa1:
        copy.wait_recv()
    times(x_far, 1 - zl, all_a, FIRST)
    zb.wait_recv()

    @pl.loop(0, 4)
    def _(xx):
        times(xx, 1 - zl, all_b, ROWS - FIRST)

    projz[...] = total[...].astype(BF)
    for s in range(4):
        start_back(projz, pr_ref, (psend, precv), s)
    deal_keep(projz, pr_ref, where)

    dz.wait_recv()
    dk_ref[...] = (three(zh, 0) + rz[0].astype(F32)).astype(BF)
    dv_ref[...] = (three(zh, 1) + rz[1].astype(F32)).astype(BF)

    deal_wait(dqz_ref, dq_ref, (gsend, grecv), where)
    deal_wait(projz, pr_ref, (psend, precv), where)
    cp.finish_sends()


def body(queries, key_input, value_input, out_weight, lengths, grad_projected):
    half_a, half_b = FIRST // 2, (ROWS - FIRST) // 2
    wide = GROUP * CHUNK
    rest = ROWS - FIRST

    def half(*dims):
        return pltpu.VMEM(dims, BF)

    def full(*dims):
        return pltpu.VMEM(dims, F32)

    def shape(*dims):
        return jax.ShapeDtypeStruct(dims, BF)

    in_vmem = pl.BlockSpec(memory_space=pltpu.VMEM)
    in_smem = pl.BlockSpec(memory_space=pltpu.SMEM)
    dma = pltpu.SemaphoreType.DMA
    return pl.pallas_call(
        layer_kernel,
        out_shape=(shape(ROWS, ROWS), shape(ROWS, ROWS), shape(ROWS, HD), shape(ROWS, HD)),
        in_specs=[in_smem] + [in_vmem] * 5,
        out_specs=(in_vmem,) * 4,
        scratch_shapes=[
            half(ROWS, ROWS), half(CTX, 2, ROWS, HD), half(HD, TOKENS), half(HD, TOKENS),
            half(ROWS, ROWS), half(ROWS, ROWS), half(ROWS, ROWS),
            half(4, 2, ROWS, ROWS), half(2, 2, half_a, ROWS), half(2, 2, FIRST, ROWS),
            half(FIRST, ROWS), half(FIRST, ROWS), half(4, rest, ROWS), half(2, half_b, ROWS),
            half(2, rest, ROWS), half(ROWS, ROWS),
            half(4, HD, wide), half(4, wide, HD), half(4, HD, wide), half(4, wide, HD),
            full(HD, wide), half(4, HD, wide), full(4, 1, wide), full(4, 1, wide),
            full(4, HD, wide), full(CTX, 2, ROWS, HD),
            half(4, 2, ROWS, ROWS), full(ROWS, ROWS), half(ROWS, ROWS),
            half(8, 2, ROWS, HD), half(8, 2, ROWS, HD), half(8, 2, ROWS, HD),
            half(2, 2, 2, ROWS // 2, HD), half(2, 2, 2, ROWS, HD), half(2, ROWS, HD), half(2, ROWS, HD),
            dma((80,)), dma((80,)),
        ] + [dma((4,))] * 8,
        compiler_params=pltpu.CompilerParams(
            collective_id=0, has_side_effects=True, vmem_limit_bytes=62 << 20
        ),
        name="layer",
    )(lengths, queries, key_input, value_input, grad_projected, out_weight)


def solution(mesh):
    both = P("ctx", "head")
    return jax.shard_map(
        body,
        mesh=mesh,
        in_specs=(both, both, both, P(None, "head"), P(), both),
        out_specs=(both, both, both, both),
        check_vma=False,
    )
```

time: 175 us -> 149 us (0.85)
  the two profiles are of different devices: /device:TPU:1 before, /device:TPU:46 now
where the time goes in v2:
time: 149 us
  Pallas kernels  141 us (95%)
  local copies, waits for them, and re-layouts  6.87 us (5%)
    pallas_call x1, Pallas kernels, body(): pl.pallas_call(layer_kernel, out_shape=(shape(ROWS, ROWS), shape(ROWS, RO...  141 us
    unnamed x4, local copies, waits for them, and re-layouts  6.87 us

profile of v2, /device:TPU:46, one launch (start us, length us, event | category | flops | bytes accessed | tf_op | source)
XLA Modules:
  0.0 148.9 jit_solution(11195872857326138305)
XLA Ops:
  0.6 141.4 %layer.1 = (bf16[512,512]{1,0:T(8,128)(2,1)}, bf16[512,512]{1,0:T(8,128)(2,1)}, bf16[512,128]{1,0:T(8,128)(2,1)}, bf16[512,128]{1,0:T(8,128)(2,1)}) custom-call(s32[6]{0:T(128)} %len_ref.1, bf16[512,512]{1,0:T(8,128)(2,1)} %q_ref.1, bf16[512,128]{1,0:T(8,128)(2,1)} %k_ref.1, bf16[512,128]{1,0:T(8,128)(2,1)} %v_ref.1, bf16[512,512]{1,0:T(8,128)(2,1)} %gp_ref.1, ...), custom_call_target="tpu_custom_call" | custom-call | tf_op jit(solution)/shard_map/layer/pallas_call | solution.py:658
  142.1 1.9 %copy.14 = bf16[512,512]{1,0:T(8,128)(2,1)} copy(bf16[512,512]{1,0:T(8,128)(2,1)} %get-tuple-element.8) | data formatting | bytes 1048576
  143.9 1.9 %copy.15 = bf16[512,512]{1,0:T(8,128)(2,1)} copy(bf16[512,512]{1,0:T(8,128)(2,1)} %get-tuple-element.9) | data formatting | bytes 1048576
  145.8 1.6 %copy.16 = bf16[512,128]{1,0:T(8,128)(2,1)} copy(bf16[512,128]{1,0:T(8,128)(2,1)} %get-tuple-element.10) | data formatting | bytes 262144
  147.4 1.6 %copy.17 = bf16[512,128]{1,0:T(8,128)(2,1)} copy(bf16[512,128]{1,0:T(8,128)(2,1)} %get-tuple-element.11) | data formatting | bytes 262144

commit v3 on v2

--- a/solution.py
+++ b/solution.py
@@ -165,7 +165,7 @@
     pr_ref, dq_ref, dk_ref, dv_ref,
     qz_ref, kv_ref, kt_ref, vt_ref, doz_ref, oz_ref, dqz_ref,
     part, ra1, ra2, raz, tz, rbz, rb1, rb2, do_own,
-    qt, qn, dot, don, ot, outs, logs, deltas, dqt, acc,
+    qt, qn, dot, don, ot, peaks, sums, outs, logs, deltas, dqt, acc,
     every, total, projz, dkv_out, rc, dsum, r1, r2, tzk, rz,
     send, recv, qsend, qrecv, dsend, drecv, gsend, grecv, psend, precv,
 ):
@@ -209,15 +209,23 @@
     up_a, lo_a = pl.ds(0, half_a), pl.ds(half_a, half_a)
     all_b = pl.ds(FIRST, 2 * half_b)
     up_b, lo_b = pl.ds(FIRST, half_b), pl.ds(FIRST + half_b, half_b)
+    pieces = FIRST // CHUNK
+    tops = [pl.ds(r * CHUNK, CHUNK // 2) for r in range(pieces)]
+    lows = [pl.ds(r * CHUNK + CHUNK // 2, CHUNK // 2) for r in range(pieces)]
+    fulls = [pl.ds(r * CHUNK, CHUNK) for r in range(pieces)]
     compute(x_far)
     a1 = [
-        cp.go(part.at[x_far, :, up_a, :], ra1.at[0], xr),
-        cp.go(part.at[x_far, :, lo_a, :], ra1.at[1], xl),
+        (
+            cp.go(part.at[x_far, :, tops[r], :], ra1.at[0, r], xr),
+            cp.go(part.at[x_far, :, lows[r], :], ra1.at[1, r], xl),
+        )
+        for r in range(pieces)
     ]
     compute(x_right)
-    a2 = [cp.go(part.at[x_right, :, lo_a, :], ra2.at[0, :, lo_a, :], xr)]
+    a2 = [[cp.go(part.at[x_right, :, lows[r], :], ra2.at[0, :, lows[r], :], xr)] for r in range(pieces)]
     compute(x_left)
-    a2.append(cp.go(part.at[x_left, :, up_a, :], ra2.at[1, :, up_a, :], xl))
+    for r in range(pieces):
+        a2[r].append(cp.go(part.at[x_left, :, tops[r], :], ra2.at[1, :, tops[r], :], xl))
     compute(x)
     bz = cp.go(part.at[:, 1 - zl, all_b, :], rbz, zp)
 
@@ -225,19 +233,6 @@
     other = kv_ref.at[slot(y, 1 - zh, core)]
     kv_y1 = [cp.go(other, other, yr), cp.go(other, other, yl)]
     mates.append(cp.go(other, other, mate))
-
-    a1[0].wait_recv()
-    for zz in range(2):
-        def put(at, n, total, zz=zz):
-            part[x_right, zz, pl.ds(at, n), :] = total.astype(BF)
-        add_rows(put, [lambda at, n, zz=zz: part[x_right, zz, pl.ds(at, n), :], lambda at, n, zz=zz: ra1[0, zz, pl.ds(at, n), :]], half_a)
-    a2.append(cp.go(part.at[x_right, :, up_a, :], ra2.at[0, :, up_a, :], xr))
-    a1[1].wait_recv()
-    for zz in range(2):
-        def put(at, n, total, zz=zz):
-            part[x_left, zz, pl.ds(half_a + at, n), :] = total.astype(BF)
-        add_rows(put, [lambda at, n, zz=zz: part[x_left, zz, pl.ds(half_a + at, n), :], lambda at, n, zz=zz: ra1[1, zz, pl.ds(at, n), :]], half_a)
-    a2.append(cp.go(part.at[x_left, :, lo_a, :], ra2.at[1, :, lo_a, :], xl))
 
     half_k = ROWS // 2
     early, late = pl.ds(0, half_k), pl.ds(half_k, half_k)
@@ -250,12 +245,148 @@
         got[1].wait_recv()
         second = kv_ref.at[from_right, :, late, :]
         forwards.append(cp.go(second, second, yl))
-        for s in (from_left, from_right):
-            mates.append(cp.go(kv_ref.at[s], kv_ref.at[s], mate))
-        return forwards
-
-    far0 = pass_on(kv_y0, zh)
-
+        swaps = [cp.go(kv_ref.at[s], kv_ref.at[s], mate) for s in (from_left, from_right)]
+        return forwards, swaps
+
+    def turn(s):
+        cols = pl.ds(pl.multiple_of(s * ROWS, ROWS), ROWS)
+        kt_ref[:, cols] = kv_ref[s, 0].T
+        vt_ref[:, cols] = kv_ref[s, 1].T
+
+    def turn_quarter(yy):
+        @pl.loop(0, 4)
+        def _(i):
+            turn(yy * 4 + i)
+
+    starts, run = [], jnp.int32(0)
+    for d in range(len_ref.shape[0]):
+        starts.append(run)
+        run = run + len_ref[d]
+    wide = GROUP * CHUNK
+
+    def place(slot):
+        odd = lax.rem(slot, 2)
+        piece = y + odd * (3 - 2 * y)
+        seat = (zh + odd * FLIP_Z * (1 - 2 * zh)) * 2 + core + odd * (1 - 2 * core)
+        return seat, (slot * 16 + seat * 4 + piece) * CHUNK
+
+    def positions(slot):
+        row0 = place(slot)[1]
+        pos = row0 + lax.rem(lax.broadcasted_iota(jnp.int32, (1, wide), 1), CHUNK)
+        begin = jnp.zeros_like(pos)
+        for at in starts:
+            begin = jnp.maximum(begin, jnp.where(at <= pos, at, 0))
+        return pos, begin
+
+    def masked_scores(j, slot, pos, begin):
+        s = jnp.dot(kv_ref[j, 0], qt[slot], preferred_element_type=F32)
+        key_pos = j * ROWS + lax.broadcasted_iota(jnp.int32, (ROWS, wide), 0)
+        seen = jnp.logical_and(key_pos <= pos, key_pos >= begin)
+        return jnp.where(seen, s, LOWEST)
+
+    def columns(j):
+        return pl.ds(pl.multiple_of(j * ROWS, ROWS), ROWS)
+
+    deal_wait(q_ref, qz_ref, (qsend, qrecv), where)
+
+    @pl.loop(0, 4)
+    def _(slot):
+        rows = pl.ds(pl.multiple_of(slot * CHUNK, CHUNK), CHUNK)
+        for h in range(GROUP):
+            block = qz_ref[rows, slice(h * HD, (h + 1) * HD)]
+            span = slice(h * CHUNK, (h + 1) * CHUNK)
+            qn[slot, span, :] = block
+            qt[slot, :, span] = block.T
+        ot[slot] = jnp.zeros(ot.shape[1:], F32)
+        peaks[slot] = jnp.full((1, wide), LOWEST, F32)
+        sums[slot] = jnp.zeros((1, wide), F32)
+
+    def units(slot, yy):
+        return jnp.where(slot == yy, place(slot)[0] + 1, 4)
+
+    def attend_quarter(yy):
+        @pl.loop(yy, 4)
+        def _(slot):
+            pos, begin = positions(slot)
+
+            def step(*blocks):
+                ss = [masked_scores(j, slot, pos, begin) for j in blocks]
+                m = peaks[slot]
+                m_new = m
+                for s in ss:
+                    m_new = jnp.maximum(m_new, jnp.max(s, axis=0, keepdims=True))
+                base = jnp.maximum(m_new, 0.5 * LOWEST)
+                scale = jnp.exp2((m - base) * TO_LOG2)
+                added = sums[slot] * scale
+                kept = ot[slot] * scale
+                for j, s in zip(blocks, ss):
+                    p = jnp.exp2((s - base) * TO_LOG2)
+                    added = added + jnp.sum(p, axis=0, keepdims=True)
+                    kept = kept + jnp.dot(vt_ref[:, columns(j)], p.astype(BF), preferred_element_type=F32)
+                ot[slot] = kept
+                peaks[slot] = m_new
+                sums[slot] = added
+
+            count = units(slot, yy)
+
+            @pl.loop(0, lax.div(count, 2))
+            def _(i):
+                step(4 * yy + 2 * i, 4 * yy + 2 * i + 1)
+
+            @pl.loop(0, lax.rem(count, 2))
+            def _(i):
+                step(4 * yy + count - 1)
+
+    def finish_slots():
+        @pl.loop(0, 4)
+        def _(slot):
+            rows = pl.ds(pl.multiple_of(slot * CHUNK, CHUNK), CHUNK)
+            out = (ot[slot] / sums[slot]).astype(BF)
+            outs[slot] = out
+            logs[slot] = peaks[slot] * TO_LOG2 + jnp.log2(sums[slot])
+            for h in range(GROUP):
+                oz_ref[rows, slice(h * HD, (h + 1) * HD)] = out[:, h * CHUNK:(h + 1) * CHUNK].T
+
+    def pass_a1(r):
+        for way, neighbour, spans, dev in ((0, x_right, tops, xr), (1, x_left, lows, xl)):
+            a1[r][way].wait_recv()
+            for zz in range(2):
+                got = ra1[way, r, zz].astype(F32)
+                part[neighbour, zz, spans[r], :] = (part[neighbour, zz, spans[r], :].astype(F32) + got).astype(BF)
+            a2[r].append(cp.go(part.at[neighbour, :, spans[r], :], ra2.at[way, :, spans[r], :], dev))
+
+    def three_a(zz, r):
+        return (
+            part[x, zz, fulls[r], :].astype(F32)
+            + ra2[0, zz, fulls[r], :].astype(F32)
+            + ra2[1, zz, fulls[r], :].astype(F32)
+        )
+
+    def sum_a(r):
+        for copy in a2[r]:
+            copy.wait_recv()
+        tz[fulls[r], :] = three_a(1 - zl, r).astype(BF)
+        return cp.go(tz.at[fulls[r], :], raz.at[fulls[r], :], zp)
+
+    def end_a(r, az):
+        az.wait_recv()
+        do_own[fulls[r], :] = (three_a(zl, r) + raz[fulls[r], :].astype(F32)).astype(BF)
+        deal_start(deal_do, r, where)
+
+    for copy in mates:
+        copy.wait_recv()
+    turn_quarter(y)
+    attend_quarter(y)
+    pass_a1(0)
+    far0, swaps0 = pass_on(kv_y0, zh)
+    far1, swaps1 = pass_on(kv_y1, 1 - zh)
+    for r in range(1, pieces):
+        pass_a1(r)
+    for copy in swaps0 + swaps1:
+        copy.wait_recv()
+    turn_quarter(y_right)
+    turn_quarter(y_left)
+    attend_quarter(y_right)
     bz.wait_recv()
 
     @pl.loop(0, 4)
@@ -270,105 +401,13 @@
         cp.go(part.at[x_right, zl, lo_b, :], rb2.at[0, pl.ds(half_b, half_b), :], xr),
         cp.go(part.at[x_left, zl, up_b, :], rb2.at[1, pl.ds(0, half_b), :], xl),
     ]
-    far1 = pass_on(kv_y1, 1 - zh)
+    last_swaps = []
     for copies, zz in ((far0, zh), (far1, 1 - zh)):
         for copy in copies:
             copy.wait_recv()
         far = kv_ref.at[slot(y_far, zz, core)]
-        mates.append(cp.go(far, far, mate))
-
-    def turn(s):
-        cols = pl.ds(pl.multiple_of(s * ROWS, ROWS), ROWS)
-        kt_ref[:, cols] = kv_ref[s, 0].T
-        vt_ref[:, cols] = kv_ref[s, 1].T
-
-    @pl.loop(0, 8)
-    def _(i):
-        turn(i * 2 + core)
-
-    for copy in mates:
-        copy.wait_recv()
-
-    @pl.loop(0, 8)
-    def _(i):
-        turn(i * 2 + 1 - core)
-
-    deal_wait(q_ref, qz_ref, (qsend, qrecv), where)
-
-    starts, run = [], jnp.int32(0)
-    for d in range(len_ref.shape[0]):
-        starts.append(run)
-        run = run + len_ref[d]
-    wide = GROUP * CHUNK
-
-    def place(slot):
-        odd = lax.rem(slot, 2)
-        piece = y + odd * (3 - 2 * y)
-        seat = (zh + odd * FLIP_Z * (1 - 2 * zh)) * 2 + core + odd * (1 - 2 * core)
-        return seat, (slot * 16 + seat * 4 + piece) * CHUNK
-
-    def positions(slot):
-        row0 = place(slot)[1]
-        pos = row0 + lax.rem(lax.broadcasted_iota(jnp.int32, (1, wide), 1), CHUNK)
-        begin = jnp.zeros_like(pos)
-        for at in starts:
-            begin = jnp.maximum(begin, jnp.where(at <= pos, at, 0))
-        return pos, begin
-
-    def masked_scores(j, slot, pos, begin):
-        s = jnp.dot(kv_ref[j, 0], qt[slot], preferred_element_type=F32)
-        key_pos = j * ROWS + lax.broadcasted_iota(jnp.int32, (ROWS, wide), 0)
-        seen = jnp.logical_and(key_pos <= pos, key_pos >= begin)
-        return jnp.where(seen, s, LOWEST)
-
-    def columns(j):
-        return pl.ds(pl.multiple_of(j * ROWS, ROWS), ROWS)
-
-    def attend_slot(slot):
-        rows = pl.ds(pl.multiple_of(slot * CHUNK, CHUNK), CHUNK)
-        for h in range(GROUP):
-            cols = slice(h * HD, (h + 1) * HD)
-            span = slice(h * CHUNK, (h + 1) * CHUNK)
-            block = qz_ref[rows, cols]
-            qn[slot, span, :] = block
-            qt[slot, :, span] = block.T
-        pos, begin = positions(slot)
-        ot[...] = jnp.zeros_like(ot)
-
-        def step(blocks, m, total):
-            ss = [masked_scores(j, slot, pos, begin) for j in blocks]
-            m_new = m
-            for s in ss:
-                m_new = jnp.maximum(m_new, jnp.max(s, axis=0, keepdims=True))
-            base = jnp.maximum(m_new, 0.5 * LOWEST)
-            scale = jnp.exp2((m - base) * TO_LOG2)
-            total = total * scale
-            kept = ot[...] * scale
-            for j, s in zip(blocks, ss):
-                p = jnp.exp2((s - base) * TO_LOG2)
-                total = total + jnp.sum(p, axis=0, keepdims=True)
-                kept = kept + jnp.dot(vt_ref[:, columns(j)], p.astype(BF), preferred_element_type=F32)
-            ot[...] = kept
-            return m_new, total
-
-        count = 4 * slot + place(slot)[0] + 1
-        carry = (jnp.full((1, wide), LOWEST, F32), jnp.zeros((1, wide), F32))
-        carry = lax.fori_loop(
-            0, lax.div(count, 2), lambda i, c: step((2 * i, 2 * i + 1), *c), carry
-        )
-        m, total = lax.fori_loop(
-            0, lax.rem(count, 2), lambda i, c: step((count - 1,), *c), carry
-        )
-        out = (ot[...] / total).astype(BF)
-        outs[slot] = out
-        logs[slot] = m * TO_LOG2 + jnp.log2(total)
-        for h in range(GROUP):
-            oz_ref[rows, slice(h * HD, (h + 1) * HD)] = out[:, h * CHUNK:(h + 1) * CHUNK].T
-
-    @pl.loop(0, 2)
-    def _(slot):
-        attend_slot(slot)
-
+        last_swaps.append(cp.go(far, far, mate))
+    attend_quarter(y_left)
     b1[0].wait_recv()
     part[x_right, zl, up_b, :] = (part[x_right, zl, up_b, :].astype(F32) + rb1[0].astype(F32)).astype(BF)
     b2.append(cp.go(part.at[x_right, zl, up_b, :], rb2.at[0, pl.ds(0, half_b), :], xr))
@@ -376,27 +415,27 @@
     part[x_left, zl, lo_b, :] = (part[x_left, zl, lo_b, :].astype(F32) + rb1[1].astype(F32)).astype(BF)
     b2.append(cp.go(part.at[x_left, zl, lo_b, :], rb2.at[1, pl.ds(half_b, half_b), :], xl))
 
-    attend_slot(jnp.int32(2))
-
-    for copy in a2:
+    for copy in last_swaps:
         copy.wait_recv()
-
-    def put_away(at, n, total):
-        tz[pl.ds(at, n), :] = total.astype(BF)
-
-    def three(zz):
-        return [
-            lambda at, n: part[x, zz, pl.ds(at, n), :],
-            lambda at, n: ra2[0, zz, pl.ds(at, n), :],
-            lambda at, n: ra2[1, zz, pl.ds(at, n), :],
-        ]
-
-    add_rows(put_away, three(1 - zl), FIRST)
-    az = cp.go(tz, raz, zp)
-
-    attend_slot(jnp.int32(3))
+    turn_quarter(y_far)
+    az = [sum_a(0)]
+    attend_quarter(y_far)
+    finish_slots()
+    for r in range(1, pieces):
+        az.append(sum_a(r))
+    all_a = pl.ds(0, FIRST)
+
+    def same(ref_at, dev):
+        return cp.go(ref_at, ref_at, dev)
+
+    every[x, zl] = oz_ref[...]
+    za = same(every.at[x, zl, all_a, :], zp)
+    b0 = [same(every.at[x, zl, all_b, :], xr), same(every.at[x, zl, all_b, :], xl)]
+    a0 = [same(every.at[x, zl, all_a, :], xr), same(every.at[x, zl, all_a, :], xl)]
 
     deal_do = deal_out(do_own, doz_ref, (dsend, drecv), where)
+    for r in range(pieces - 1):
+        end_a(r, az[r])
     for copy in b2:
         copy.wait_recv()
 
@@ -413,24 +452,7 @@
         ROWS - FIRST,
     )
     deal_start(deal_do, 3, where)
-
-    all_a = pl.ds(0, FIRST)
-    def same(ref_at, dev):
-        return cp.go(ref_at, ref_at, dev)
-
-    every[x, zl] = oz_ref[...]
-    za = same(every.at[x, zl, all_a, :], zp)
-    b0 = [same(every.at[x, zl, all_b, :], xr), same(every.at[x, zl, all_b, :], xl)]
-    a0 = [same(every.at[x, zl, all_a, :], xr), same(every.at[x, zl, all_a, :], xl)]
-
-    az.wait_recv()
-
-    def put_a(at, n, total):
-        do_own[pl.ds(at, n), :] = total.astype(BF)
-
-    add_rows(put_a, three(zl) + [lambda at, n: raz[pl.ds(at, n), :]], FIRST)
-    for r in range(3):
-        deal_start(deal_do, r, where)
+    end_a(pieces - 1, az[pieces - 1])
     deal_keep(do_own, doz_ref, where)
 
     def deal_back(src, dst, sems, slot):
@@ -496,7 +518,7 @@
                 acc[j, 0] += jnp.dot(ds, qn[slot], preferred_element_type=F32)
                 dqt[slot] += jnp.dot(kt_ref[:, columns(j)], ds, preferred_element_type=F32)
 
-            count = jnp.where(slot == yy, place(slot)[0] + 1, 4)
+            count = units(slot, yy)
 
             @pl.loop(0, lax.div(count, 2))
             def _(i):
@@ -564,21 +586,8 @@
 
     times(x_left, 1 - zl, all_a, FIRST)
     times(x_right, 1 - zl, all_a, FIRST)
-    swap_own = sweep_quarter(y)
-
-    @pl.loop(0, 4)
-    def _(slot):
-        rows = pl.ds(pl.multiple_of(slot * CHUNK, CHUNK), CHUNK)
-        grads = (dqt[slot] * INV_ROOT).astype(BF)
-        for h in range(GROUP):
-            dqz_ref[rows, slice(h * HD, (h + 1) * HD)] = grads[:, h * CHUNK:(h + 1) * CHUNK].T
-
     join(y_left, swap_left)
     d2.append(cp.go(dsum.at[pair(y_left), :, early, :], r2.at[1, :, :, early, :], yl))
-    for s in range(4):
-        start_back(dqz_ref, dq_ref, (gsend, grecv), s)
-    deal_keep(dqz_ref, dq_ref, where)
-
     d1[0].wait_recv()
 
     def add_into(zz, kind, which, yy, rows):
@@ -596,10 +605,22 @@
             add_into(zz, kind, 1, y_left, late)
     d2.append(cp.go(dsum.at[pair(y_left), :, late, :], r2.at[1, :, :, late, :], yl))
 
+    swap_own = sweep_quarter(y)
+
+    @pl.loop(0, 4)
+    def _(slot):
+        rows = pl.ds(pl.multiple_of(slot * CHUNK, CHUNK), CHUNK)
+        grads = (dqt[slot] * INV_ROOT).astype(BF)
+        for h in range(GROUP):
+            dqz_ref[rows, slice(h * HD, (h + 1) * HD)] = grads[:, h * CHUNK:(h + 1) * CHUNK].T
+
+    for s in range(4):
+        start_back(dqz_ref, dq_ref, (gsend, grecv), s)
+    deal_keep(dqz_ref, dq_ref, where)
+
     for copy in fa0:
         copy.wait_recv()
     times(x_far, zl, pl.ds(0, ROWS), ROWS)
-
     join(y, swap_own)
     for copy in d2:
         copy.wait_recv()
@@ -614,18 +635,20 @@
     for kind in range(2):
         tzk[kind] = three(1 - zh, kind).astype(BF)
     dz = cp.go(tzk, rz, hp)
-
     for copy in fa1:
         copy.wait_recv()
     times(x_far, 1 - zl, all_a, FIRST)
+    projz[all_a, :] = total[all_a, :].astype(BF)
+    for s in range(pieces):
+        start_back(projz, pr_ref, (psend, precv), s)
     zb.wait_recv()
 
     @pl.loop(0, 4)
     def _(xx):
         times(xx, 1 - zl, all_b, ROWS - FIRST)
 
-    projz[...] = total[...].astype(BF)
-    for s in range(4):
+    projz[all_b, :] = total[all_b, :].astype(BF)
+    for s in range(pieces, 4):
         start_back(projz, pr_ref, (psend, precv), s)
     deal_keep(projz, pr_ref, where)
 
@@ -638,8 +661,17 @@
     cp.finish_sends()
 
 
+def hand_over(*refs):
+    sources, targets, done = refs[:4], refs[4:8], refs[8]
+    copies = [pltpu.make_async_copy(a, b, done.at[i]) for i, (a, b) in enumerate(zip(sources, targets))]
+    for copy in copies:
+        copy.start()
+    for copy in copies:
+        copy.wait()
+
+
 def body(queries, key_input, value_input, out_weight, lengths, grad_projected):
-    half_a, half_b = FIRST // 2, (ROWS - FIRST) // 2
+    half_b = (ROWS - FIRST) // 2
     wide = GROUP * CHUNK
     rest = ROWS - FIRST
 
@@ -655,7 +687,7 @@
     in_vmem = pl.BlockSpec(memory_space=pltpu.VMEM)
     in_smem = pl.BlockSpec(memory_space=pltpu.SMEM)
     dma = pltpu.SemaphoreType.DMA
-    return pl.pallas_call(
+    outputs = pl.pallas_call(
         layer_kernel,
         out_shape=(shape(ROWS, ROWS), shape(ROWS, ROWS), shape(ROWS, HD), shape(ROWS, HD)),
         in_specs=[in_smem] + [in_vmem] * 5,
@@ -663,22 +695,31 @@
         scratch_shapes=[
             half(ROWS, ROWS), half(CTX, 2, ROWS, HD), half(HD, TOKENS), half(HD, TOKENS),
             half(ROWS, ROWS), half(ROWS, ROWS), half(ROWS, ROWS),
-            half(4, 2, ROWS, ROWS), half(2, 2, half_a, ROWS), half(2, 2, FIRST, ROWS),
+            half(4, 2, ROWS, ROWS), half(2, FIRST // CHUNK, 2, CHUNK // 2, ROWS), half(2, 2, FIRST, ROWS),
             half(FIRST, ROWS), half(FIRST, ROWS), half(4, rest, ROWS), half(2, half_b, ROWS),
             half(2, rest, ROWS), half(ROWS, ROWS),
             half(4, HD, wide), half(4, wide, HD), half(4, HD, wide), half(4, wide, HD),
-            full(HD, wide), half(4, HD, wide), full(4, 1, wide), full(4, 1, wide),
+            full(4, HD, wide), full(4, 1, wide), full(4, 1, wide), half(4, HD, wide), full(4, 1, wide), full(4, 1, wide),
             full(4, HD, wide), full(CTX, 2, ROWS, HD),
             half(4, 2, ROWS, ROWS), full(ROWS, ROWS), half(ROWS, ROWS),
             half(8, 2, ROWS, HD), half(8, 2, ROWS, HD), half(8, 2, ROWS, HD),
             half(2, 2, 2, ROWS // 2, HD), half(2, 2, 2, ROWS, HD), half(2, ROWS, HD), half(2, ROWS, HD),
-            dma((80,)), dma((80,)),
+            dma((96,)), dma((96,)),
         ] + [dma((4,))] * 8,
         compiler_params=pltpu.CompilerParams(
             collective_id=0, has_side_effects=True, vmem_limit_bytes=62 << 20
         ),
         name="layer",
     )(lengths, queries, key_input, value_input, grad_projected, out_weight)
+    anywhere = pl.BlockSpec(memory_space=pl.ANY)
+    return pl.pallas_call(
+        hand_over,
+        out_shape=(shape(ROWS, ROWS), shape(ROWS, ROWS), shape(ROWS, HD), shape(ROWS, HD)),
+        in_specs=[anywhere] * 4,
+        out_specs=(anywhere,) * 4,
+        scratch_shapes=[dma((4,))],
+        name="hand_over",
+    )(*outputs)
 
 
 def solution(mesh):

time: 149 us -> 179 us (1.20)
  the two profiles are of different devices: /device:TPU:46 before, /device:TPU:9 now
where the time goes in v3:
time: 179 us; the launch traced here: 178 us
  Pallas kernels  178 us (99%)
    pallas_call x1, Pallas kernels, body(): pl.pallas_call(layer_kernel, out_shape=(shape(ROWS, ROWS), shape(ROWS, RO...  137 us
    pallas_call x1, Pallas kernels, body(): pl.pallas_call(hand_over, out_shape=(shape(ROWS, ROWS), shape(ROWS, ROWS)...  40.8 us

profile of v3, /device:TPU:9, one launch (start us, length us, event | category | flops | bytes accessed | tf_op | source)
XLA Modules:
  0.0 178.4 jit_solution(12507070304515506947)
XLA Ops:
  0.6 136.8 %layer.1 = (bf16[512,512]{1,0:T(8,128)(2,1)}, bf16[512,512]{1,0:T(8,128)(2,1)}, bf16[512,128]{1,0:T(8,128)(2,1)}, bf16[512,128]{1,0:T(8,128)(2,1)}) custom-call(s32[6]{0:T(128)} %len_ref.1, bf16[512,512]{1,0:T(8,128)(2,1)} %q_ref.1, bf16[512,128]{1,0:T(8,128)(2,1)} %k_ref.1, bf16[512,128]{1,0:T(8,128)(2,1)} %v_ref.1, bf16[512,512]{1,0:T(8,128)(2,1)} %gp_ref.1, ...), custom_call_target="tpu_custom_call" | custom-call | tf_op jit(solution)/shard_map/layer/pallas_call | solution.py:690
  137.4 40.8 %hand_over.1 = (bf16[512,512]{1,0:T(8,128)(2,1)}, bf16[512,512]{1,0:T(8,128)(2,1)}, bf16[512,128]{1,0:T(8,128)(2,1)}, bf16[512,128]{1,0:T(8,128)(2,1)}) custom-call(bf16[512,512]{1,0:T(8,128)(2,1)} %get-tuple-element.8.refs_0_, bf16[512,512]{1,0:T(8,128)(2,1)} %get-tuple-element.9.refs_1_, bf16[512,128]{1,0:T(8,128)(2,1)} %get-tuple-element.10.refs_2_, ...), custom_call_target="tpu_custom_call" | custom-call | tf_op jit(solution)/shard_map/hand_over/pallas_call | solution.py:715

commit v4 on v3

--- a/solution.py
+++ b/solution.py
@@ -7,6 +7,7 @@
 from jax.experimental.pallas import tpu as pltpu
 from jax.sharding import PartitionSpec as P
 
+QH = 32
 HD = 128
 GROUP = 4
 ROWS = 512
@@ -161,17 +162,19 @@
 
 
 def layer_kernel(
-    len_ref, q_ref, k_ref, v_ref, gp_ref, w_ref,
+    len_ref, q_ref, k_ref, v_ref, gp_ref, w_hbm,
     pr_ref, dq_ref, dk_ref, dv_ref,
     qz_ref, kv_ref, kt_ref, vt_ref, doz_ref, oz_ref, dqz_ref,
     part, ra1, ra2, raz, tz, rbz, rb1, rb2, do_own,
     qt, qn, dot, don, ot, peaks, sums, outs, logs, deltas, dqt, acc,
     every, total, projz, dkv_out, rc, dsum, r1, r2, tzk, rz,
-    send, recv, qsend, qrecv, dsend, drecv, gsend, grecv, psend, precv,
+    send, recv, qsend, qrecv, dsend, drecv, gsend, grecv, psend, precv, w_ref, wsem,
 ):
     where = coords()
     y, zh, core, zl, x = where
     c = y * 4 + zh * 2 + core
+    weights = pltpu.make_async_copy(w_hbm, w_ref, wsem)
+    weights.start()
     greet(*where)
     cp = Copies(send, recv)
     xr, xl = device(y, zh, core, zl, around(x + 1)), device(y, zh, core, zl, around(x - 1))
@@ -213,6 +216,7 @@
     tops = [pl.ds(r * CHUNK, CHUNK // 2) for r in range(pieces)]
     lows = [pl.ds(r * CHUNK + CHUNK // 2, CHUNK // 2) for r in range(pieces)]
     fulls = [pl.ds(r * CHUNK, CHUNK) for r in range(pieces)]
+    weights.wait()
     compute(x_far)
     a1 = [
         (
@@ -278,15 +282,46 @@
             begin = jnp.maximum(begin, jnp.where(at <= pos, at, 0))
         return pos, begin
 
-    def masked_scores(j, slot, pos, begin):
+    def masked_scores(j, slot, pos, begin, last):
         s = jnp.dot(kv_ref[j, 0], qt[slot], preferred_element_type=F32)
-        key_pos = j * ROWS + lax.broadcasted_iota(jnp.int32, (ROWS, wide), 0)
-        seen = jnp.logical_and(key_pos <= pos, key_pos >= begin)
+        key = lax.broadcasted_iota(jnp.int32, (ROWS, wide), 0)
+        seen = key >= begin - j * ROWS
+        if last:
+            seen = jnp.logical_and(seen, key <= pos - j * ROWS)
         return jnp.where(seen, s, LOWEST)
 
     def columns(j):
         return pl.ds(pl.multiple_of(j * ROWS, ROWS), ROWS)
 
+    def pass_a1(r):
+        for way, neighbour, spans, dev in ((0, x_right, tops, xr), (1, x_left, lows, xl)):
+            a1[r][way].wait_recv()
+            for zz in range(2):
+                got = ra1[way, r, zz].astype(F32)
+                part[neighbour, zz, spans[r], :] = (part[neighbour, zz, spans[r], :].astype(F32) + got).astype(BF)
+            a2[r].append(cp.go(part.at[neighbour, :, spans[r], :], ra2.at[way, :, spans[r], :], dev))
+
+    def three_a(zz, r):
+        return (
+            part[x, zz, fulls[r], :].astype(F32)
+            + ra2[0, zz, fulls[r], :].astype(F32)
+            + ra2[1, zz, fulls[r], :].astype(F32)
+        )
+
+    def sum_a(r):
+        for copy in a2[r]:
+            copy.wait_recv()
+        tz[fulls[r], :] = three_a(1 - zl, r).astype(BF)
+        return cp.go(tz.at[fulls[r], :], raz.at[fulls[r], :], zp)
+
+    def end_a(r, az):
+        az.wait_recv()
+        do_own[fulls[r], :] = (three_a(zl, r) + raz[fulls[r], :].astype(F32)).astype(BF)
+        deal_start(deal_do, r, where)
+
+    far0, swaps0 = pass_on(kv_y0, zh)
+    for r in range(pieces - 1):
+        pass_a1(r)
     deal_wait(q_ref, qz_ref, (qsend, qrecv), where)
 
     @pl.loop(0, 4)
@@ -301,16 +336,29 @@
         peaks[slot] = jnp.full((1, wide), LOWEST, F32)
         sums[slot] = jnp.zeros((1, wide), F32)
 
-    def units(slot, yy):
-        return jnp.where(slot == yy, place(slot)[0] + 1, 4)
+    def over_blocks(slot, yy, step):
+        own = slot == yy
+        count = jnp.where(own, place(slot)[0], 4)
+
+        @pl.loop(0, lax.div(count, 2))
+        def _(i):
+            step(False, 4 * yy + 2 * i, 4 * yy + 2 * i + 1)
+
+        @pl.loop(0, lax.rem(count, 2))
+        def _(i):
+            step(False, 4 * yy + count - 1)
+
+        @pl.loop(0, jnp.where(own, 1, 0))
+        def _(i):
+            step(True, 4 * yy + count)
 
     def attend_quarter(yy):
         @pl.loop(yy, 4)
         def _(slot):
             pos, begin = positions(slot)
 
-            def step(*blocks):
-                ss = [masked_scores(j, slot, pos, begin) for j in blocks]
+            def step(last, *blocks):
+                ss = [masked_scores(j, slot, pos, begin, last) for j in blocks]
                 m = peaks[slot]
                 m_new = m
                 for s in ss:
@@ -327,15 +375,7 @@
                 peaks[slot] = m_new
                 sums[slot] = added
 
-            count = units(slot, yy)
-
-            @pl.loop(0, lax.div(count, 2))
-            def _(i):
-                step(4 * yy + 2 * i, 4 * yy + 2 * i + 1)
-
-            @pl.loop(0, lax.rem(count, 2))
-            def _(i):
-                step(4 * yy + count - 1)
+            over_blocks(slot, yy, step)
 
     def finish_slots():
         @pl.loop(0, 4)
@@ -347,41 +387,12 @@
             for h in range(GROUP):
                 oz_ref[rows, slice(h * HD, (h + 1) * HD)] = out[:, h * CHUNK:(h + 1) * CHUNK].T
 
-    def pass_a1(r):
-        for way, neighbour, spans, dev in ((0, x_right, tops, xr), (1, x_left, lows, xl)):
-            a1[r][way].wait_recv()
-            for zz in range(2):
-                got = ra1[way, r, zz].astype(F32)
-                part[neighbour, zz, spans[r], :] = (part[neighbour, zz, spans[r], :].astype(F32) + got).astype(BF)
-            a2[r].append(cp.go(part.at[neighbour, :, spans[r], :], ra2.at[way, :, spans[r], :], dev))
-
-    def three_a(zz, r):
-        return (
-            part[x, zz, fulls[r], :].astype(F32)
-            + ra2[0, zz, fulls[r], :].astype(F32)
-            + ra2[1, zz, fulls[r], :].astype(F32)
-        )
-
-    def sum_a(r):
-        for copy in a2[r]:
-            copy.wait_recv()
-        tz[fulls[r], :] = three_a(1 - zl, r).astype(BF)
-        return cp.go(tz.at[fulls[r], :], raz.at[fulls[r], :], zp)
-
-    def end_a(r, az):
-        az.wait_recv()
-        do_own[fulls[r], :] = (three_a(zl, r) + raz[fulls[r], :].astype(F32)).astype(BF)
-        deal_start(deal_do, r, where)
-
     for copy in mates:
         copy.wait_recv()
     turn_quarter(y)
+    pass_a1(pieces - 1)
     attend_quarter(y)
-    pass_a1(0)
-    far0, swaps0 = pass_on(kv_y0, zh)
     far1, swaps1 = pass_on(kv_y1, 1 - zh)
-    for r in range(1, pieces):
-        pass_a1(r)
     for copy in swaps0 + swaps1:
         copy.wait_recv()
     turn_quarter(y_right)
@@ -509,8 +520,8 @@
             pos, begin = positions(slot)
             log_total, delta = logs[slot], deltas[slot]
 
-            def unit(j):
-                s = masked_scores(j, slot, pos, begin)
+            def unit(j, last):
+                s = masked_scores(j, slot, pos, begin, last)
                 dp = jnp.dot(kv_ref[j, 1], dot[slot], preferred_element_type=F32)
                 p = jnp.exp2(s * TO_LOG2 - log_total)
                 ds = (p * (dp - delta)).astype(BF)
@@ -518,16 +529,11 @@
                 acc[j, 0] += jnp.dot(ds, qn[slot], preferred_element_type=F32)
                 dqt[slot] += jnp.dot(kt_ref[:, columns(j)], ds, preferred_element_type=F32)
 
-            count = units(slot, yy)
-
-            @pl.loop(0, lax.div(count, 2))
-            def _(i):
-                unit(4 * yy + 2 * i)
-                unit(4 * yy + 2 * i + 1)
-
-            @pl.loop(0, lax.rem(count, 2))
-            def _(i):
-                unit(4 * yy + count - 1)
+            def step(last, *blocks):
+                for j in blocks:
+                    unit(j, last)
+
+            over_blocks(slot, yy, step)
 
         @pl.loop(0, 2)
         def _(zz):
@@ -551,7 +557,6 @@
             dsum[mine, 0] = (acc[j, 0] * INV_ROOT + rc[mine, 0].astype(F32)).astype(BF)
             dsum[mine, 1] = (acc[j, 1] + rc[mine, 1].astype(F32)).astype(BF)
 
-    swap_far = sweep_quarter(y_far)
     za.wait_recv()
     a1 = [same(every.at[x, 1 - zl, all_a, :], xr), same(every.at[x, 1 - zl, all_a, :], xl)]
     b0[0].wait_recv()
@@ -562,6 +567,7 @@
     fa0 = [same(every.at[x_left, zl, up_a, :], xr)]
     a0[1].wait_recv()
     fa0.append(same(every.at[x_right, zl, lo_a, :], xl))
+    swap_far = sweep_quarter(y_far)
     times(x, 1 - zl, all_a, FIRST)
 
     swap_right = sweep_quarter(y_right)
@@ -605,6 +611,9 @@
             add_into(zz, kind, 1, y_left, late)
     d2.append(cp.go(dsum.at[pair(y_left), :, late, :], r2.at[1, :, :, late, :], yl))
 
+    for copy in fa0:
+        copy.wait_recv()
+    times(x_far, zl, pl.ds(0, ROWS), ROWS)
     swap_own = sweep_quarter(y)
 
     @pl.loop(0, 4)
@@ -618,9 +627,6 @@
         start_back(dqz_ref, dq_ref, (gsend, grecv), s)
     deal_keep(dqz_ref, dq_ref, where)
 
-    for copy in fa0:
-        copy.wait_recv()
-    times(x_far, zl, pl.ds(0, ROWS), ROWS)
     join(y, swap_own)
     for copy in d2:
         copy.wait_recv()
@@ -662,12 +668,8 @@
 
 
 def hand_over(*refs):
-    sources, targets, done = refs[:4], refs[4:8], refs[8]
-    copies = [pltpu.make_async_copy(a, b, done.at[i]) for i, (a, b) in enumerate(zip(sources, targets))]
-    for copy in copies:
-        copy.start()
-    for copy in copies:
-        copy.wait()
+    for source, target in zip(refs[:4], refs[4:]):
+        target[...] = source[...]
 
 
 def body(queries, key_input, value_input, out_weight, lengths, grad_projected):
@@ -690,7 +692,7 @@
     outputs = pl.pallas_call(
         layer_kernel,
         out_shape=(shape(ROWS, ROWS), shape(ROWS, ROWS), shape(ROWS, HD), shape(ROWS, HD)),
-        in_specs=[in_smem] + [in_vmem] * 5,
+        in_specs=[in_smem] + [in_vmem] * 4 + [pl.BlockSpec(memory_space=pl.ANY)],
         out_specs=(in_vmem,) * 4,
         scratch_shapes=[
             half(ROWS, ROWS), half(CTX, 2, ROWS, HD), half(HD, TOKENS), half(HD, TOKENS),
@@ -705,19 +707,17 @@
             half(8, 2, ROWS, HD), half(8, 2, ROWS, HD), half(8, 2, ROWS, HD),
             half(2, 2, 2, ROWS // 2, HD), half(2, 2, 2, ROWS, HD), half(2, ROWS, HD), half(2, ROWS, HD),
             dma((96,)), dma((96,)),
-        ] + [dma((4,))] * 8,
+        ] + [dma((4,))] * 8 + [half(QH * HD, ROWS), dma],
         compiler_params=pltpu.CompilerParams(
             collective_id=0, has_side_effects=True, vmem_limit_bytes=62 << 20
         ),
         name="layer",
     )(lengths, queries, key_input, value_input, grad_projected, out_weight)
-    anywhere = pl.BlockSpec(memory_space=pl.ANY)
     return pl.pallas_call(
         hand_over,
         out_shape=(shape(ROWS, ROWS), shape(ROWS, ROWS), shape(ROWS, HD), shape(ROWS, HD)),
-        in_specs=[anywhere] * 4,
-        out_specs=(anywhere,) * 4,
-        scratch_shapes=[dma((4,))],
+        in_specs=[in_vmem] * 4,
+        out_specs=(in_vmem,) * 4,
         name="hand_over",
     )(*outputs)
 

time: 179 us -> 131 us (0.73)
  the two profiles are of different devices: /device:TPU:9 before, /device:TPU:1 now
where the time goes in v4:
time: 131 us
  Pallas kernels  130 us (99%)
    pallas_call x1, Pallas kernels, body(): pl.pallas_call(layer_kernel, out_shape=(shape(ROWS, ROWS), shape(ROWS, RO...  128 us

profile of v4, /device:TPU:1, one launch (start us, length us, event | category | flops | bytes accessed | tf_op | source)
XLA Modules:
  0.0 131.0 jit_solution(1709322712285169951)
XLA Ops:
  0.6 128.0 %layer.1 = (bf16[512,512]{1,0:T(8,128)(2,1)}, bf16[512,512]{1,0:T(8,128)(2,1)}, bf16[512,128]{1,0:T(8,128)(2,1)}, bf16[512,128]{1,0:T(8,128)(2,1)}) custom-call(s32[6]{0:T(128)} %len_ref.1, bf16[512,512]{1,0:T(8,128)(2,1)} %q_ref.1, bf16[512,128]{1,0:T(8,128)(2,1)} %k_ref.1, bf16[512,128]{1,0:T(8,128)(2,1)} %v_ref.1, bf16[512,512]{1,0:T(8,128)(2,1)} %gp_ref.1, ...), custom_call_target="tpu_custom_call" | custom-call | tf_op jit(solution)/shard_map/layer/pallas_call | solution.py:692
  128.7 2.3 %hand_over.1 = (bf16[512,512]{1,0:T(8,128)(2,1)}, bf16[512,512]{1,0:T(8,128)(2,1)}, bf16[512,128]{1,0:T(8,128)(2,1)}, bf16[512,128]{1,0:T(8,128)(2,1)}) custom-call(bf16[512,512]{1,0:T(8,128)(2,1)} %get-tuple-element.8.refs_0_, bf16[512,512]{1,0:T(8,128)(2,1)} %get-tuple-element.9.refs_1_, bf16[512,128]{1,0:T(8,128)(2,1)} %get-tuple-element.10.refs_2_, ...), custom_call_target="tpu_custom_call" | custom-call | tf_op jit(solution)/shard_map/hand_over/pallas_call | solution.py:716

commit v5 on v4

--- a/solution.py
+++ b/solution.py
@@ -87,7 +87,7 @@
         peers.append({"ctx": lax.rem(c + step, CTX), "head": zl * 4 + x})
     for peer in peers:
         pl.semaphore_signal(barrier, inc=1, device_id=peer, device_id_type=MESH)
-    pl.semaphore_wait(barrier, len(peers))
+    return lambda: pl.semaphore_wait(barrier, len(peers))
 
 
 def deal_out(src, dst, sems, where):
@@ -175,7 +175,7 @@
     c = y * 4 + zh * 2 + core
     weights = pltpu.make_async_copy(w_hbm, w_ref, wsem)
     weights.start()
-    greet(*where)
+    all_here = greet(*where)
     cp = Copies(send, recv)
     xr, xl = device(y, zh, core, zl, around(x + 1)), device(y, zh, core, zl, around(x - 1))
     zp = device(y, zh, core, 1 - zl, x)
@@ -191,16 +191,6 @@
 
     kv_ref[c, 0] = k_ref[...]
     kv_ref[c, 1] = v_ref[...]
-    own = kv_ref.at[c]
-    kv_z = cp.go(own, own, hp)
-    kv_y0 = [cp.go(own, own, yr), cp.go(own, own, yl)]
-    mates = [cp.go(own, own, mate)]
-    deal_q = deal_out(q_ref, qz_ref, (qsend, qrecv), where)
-
-    for r in range(4):
-        deal_start(deal_q, r, where)
-    deal_keep(q_ref, qz_ref, where)
-
     def compute(xx):
         @pl.loop(0, 2)
         def _(zz):
@@ -209,6 +199,17 @@
                 gp_ref[...], w_ref[rows, :], (((1,), (1,)), ((), ())), preferred_element_type=F32
             ).astype(BF)
 
+    weights.wait()
+    compute(x_far)
+    all_here()
+    own = kv_ref.at[c]
+    kv_z = cp.go(own, own, hp)
+    kv_y0 = [cp.go(own, own, yr), cp.go(own, own, yl)]
+    mates = [cp.go(own, own, mate)]
+    deal_q = deal_out(q_ref, qz_ref, (qsend, qrecv), where)
+    for r in range(4):
+        deal_start(deal_q, r, where)
+
     up_a, lo_a = pl.ds(0, half_a), pl.ds(half_a, half_a)
     all_b = pl.ds(FIRST, 2 * half_b)
     up_b, lo_b = pl.ds(FIRST, half_b), pl.ds(FIRST + half_b, half_b)
@@ -216,8 +217,6 @@
     tops = [pl.ds(r * CHUNK, CHUNK // 2) for r in range(pieces)]
     lows = [pl.ds(r * CHUNK + CHUNK // 2, CHUNK // 2) for r in range(pieces)]
     fulls = [pl.ds(r * CHUNK, CHUNK) for r in range(pieces)]
-    weights.wait()
-    compute(x_far)
     a1 = [
         (
             cp.go(part.at[x_far, :, tops[r], :], ra1.at[0, r], xr),
@@ -231,6 +230,7 @@
     for r in range(pieces):
         a2[r].append(cp.go(part.at[x_left, :, tops[r], :], ra2.at[1, :, tops[r], :], xl))
     compute(x)
+    deal_keep(q_ref, qz_ref, where)
     bz = cp.go(part.at[:, 1 - zl, all_b, :], rbz, zp)
 
     kv_z.wait_recv()
@@ -412,13 +412,13 @@
         cp.go(part.at[x_right, zl, lo_b, :], rb2.at[0, pl.ds(half_b, half_b), :], xr),
         cp.go(part.at[x_left, zl, up_b, :], rb2.at[1, pl.ds(0, half_b), :], xl),
     ]
+    attend_quarter(y_left)
     last_swaps = []
     for copies, zz in ((far0, zh), (far1, 1 - zh)):
         for copy in copies:
             copy.wait_recv()
         far = kv_ref.at[slot(y_far, zz, core)]
         last_swaps.append(cp.go(far, far, mate))
-    attend_quarter(y_left)
     b1[0].wait_recv()
     part[x_right, zl, up_b, :] = (part[x_right, zl, up_b, :].astype(F32) + rb1[0].astype(F32)).astype(BF)
     b2.append(cp.go(part.at[x_right, zl, up_b, :], rb2.at[0, pl.ds(0, half_b), :], xr))
@@ -426,14 +426,12 @@
     part[x_left, zl, lo_b, :] = (part[x_left, zl, lo_b, :].astype(F32) + rb1[1].astype(F32)).astype(BF)
     b2.append(cp.go(part.at[x_left, zl, lo_b, :], rb2.at[1, pl.ds(half_b, half_b), :], xl))
 
+    az = [sum_a(r) for r in range(pieces)]
     for copy in last_swaps:
         copy.wait_recv()
     turn_quarter(y_far)
-    az = [sum_a(0)]
     attend_quarter(y_far)
     finish_slots()
-    for r in range(1, pieces):
-        az.append(sum_a(r))
     all_a = pl.ds(0, FIRST)
 
     def same(ref_at, dev):
@@ -557,25 +555,29 @@
             dsum[mine, 0] = (acc[j, 0] * INV_ROOT + rc[mine, 0].astype(F32)).astype(BF)
             dsum[mine, 1] = (acc[j, 1] + rc[mine, 1].astype(F32)).astype(BF)
 
-    za.wait_recv()
-    a1 = [same(every.at[x, 1 - zl, all_a, :], xr), same(every.at[x, 1 - zl, all_a, :], xl)]
     b0[0].wait_recv()
     fb = [same(every.at[x_left, zl, up_b, :], xr)]
     b0[1].wait_recv()
     fb.append(same(every.at[x_right, zl, lo_b, :], xl))
+    za.wait_recv()
+    a1 = [same(every.at[x, 1 - zl, all_a, :], xr), same(every.at[x, 1 - zl, all_a, :], xl)]
     a0[0].wait_recv()
     fa0 = [same(every.at[x_left, zl, up_a, :], xr)]
     a0[1].wait_recv()
     fa0.append(same(every.at[x_right, zl, lo_a, :], xl))
     swap_far = sweep_quarter(y_far)
+    for copy in fb:
+        copy.wait_recv()
+    zb = same(every.at[:, zl, all_b, :], zp)
     times(x, 1 - zl, all_a, FIRST)
 
-    swap_right = sweep_quarter(y_right)
     join(y_far, swap_far)
     d1 = [
         cp.go(dsum.at[pair(y_far), :, early, :], r1.at[0], yr),
         cp.go(dsum.at[pair(y_far), :, late, :], r1.at[1], yl),
     ]
+
+    swap_right = sweep_quarter(y_right)
     a1[0].wait_recv()
     fa1 = [same(every.at[x_left, 1 - zl, up_a, :], xr)]
     a1[1].wait_recv()
@@ -586,9 +588,6 @@
     swap_left = sweep_quarter(y_left)
     join(y_right, swap_right)
     d2 = [cp.go(dsum.at[pair(y_right), :, late, :], r2.at[0, :, :, late, :], yr)]
-    for copy in fb:
-        copy.wait_recv()
-    zb = same(every.at[:, zl, all_b, :], zp)
 
     times(x_left, 1 - zl, all_a, FIRST)
     times(x_right, 1 - zl, all_a, FIRST)

time: 131 us -> 132 us (level)
  Pallas kernels: 130 us -> 132 us
where the time goes in v5:
time: 132 us
  Pallas kernels  132 us (100%)
    pallas_call x1, Pallas kernels, body(): pl.pallas_call(layer_kernel, out_shape=(shape(ROWS, ROWS), shape(ROWS, RO...  129 us

profile of v5, /device:TPU:1, one launch (start us, length us, event | category | flops | bytes accessed | tf_op | source)
XLA Modules:
  0.0 132.2 jit_solution(14411184768519696391)
XLA Ops:
  0.6 129.3 %layer.1 = (bf16[512,512]{1,0:T(8,128)(2,1)}, bf16[512,512]{1,0:T(8,128)(2,1)}, bf16[512,128]{1,0:T(8,128)(2,1)}, bf16[512,128]{1,0:T(8,128)(2,1)}) custom-call(s32[6]{0:T(128)} %len_ref.1, bf16[512,512]{1,0:T(8,128)(2,1)} %q_ref.1, bf16[512,128]{1,0:T(8,128)(2,1)} %k_ref.1, bf16[512,128]{1,0:T(8,128)(2,1)} %v_ref.1, bf16[512,512]{1,0:T(8,128)(2,1)} %gp_ref.1, ...), custom_call_target="tpu_custom_call" | custom-call | tf_op jit(solution)/shard_map/layer/pallas_call | solution.py:691
  129.9 2.3 %hand_over.1 = (bf16[512,512]{1,0:T(8,128)(2,1)}, bf16[512,512]{1,0:T(8,128)(2,1)}, bf16[512,128]{1,0:T(8,128)(2,1)}, bf16[512,128]{1,0:T(8,128)(2,1)}) custom-call(bf16[512,512]{1,0:T(8,128)(2,1)} %get-tuple-element.8.refs_0_, bf16[512,512]{1,0:T(8,128)(2,1)} %get-tuple-element.9.refs_1_, bf16[512,128]{1,0:T(8,128)(2,1)} %get-tuple-element.10.refs_2_, ...), custom_call_target="tpu_custom_call" | custom-call | tf_op jit(solution)/shard_map/hand_over/pallas_call | solution.py:715
